TPU v7x, 32 devices: a whole 2x2x4 slice. The times are simulated.
32 devices in a mesh: row: 16 (over z, y, x), col: 2 (over core).
Axes of the slice: x: 2, y: 2, z: 4, core: 2. Of those that a mesh axis runs over, the one named last changes fastest.
Arguments:
- frames: bfloat16 [4, 4096, 2048], P(None, 'row', 'col'), may hold values from -6 to 6
- row_factor: bfloat16 [4096, 256], P('row')
- col_factor: bfloat16 [2048, 256], P('col')
- row_history: float32 [4096, 256], P('row'), may hold values from -8 to 8
- col_history: float32 [2048, 256], P('col'), may hold values from -8 to 8
- time_gram: float32 [256, 256], replicated, as said below
Outputs:
- frame_factor: float32 [4, 256], replicated
- new_row_factor: bfloat16 [4096, 256], P('row')
- new_col_factor: bfloat16 [2048, 256], P('col')
Inputs may be any that keep to these rules, and one draw needn't show every extreme that they name: `time_gram`: symmetric positive definite.
All inputs are finite; a program needn't handle non-finite values.
Results may differ from a plain program's by a relative error of at most 0.0041.
Values may be sent and summed in bfloat16 or wider, within the bound.
A program may use at most 64 MiB of HBM per device.

v0:
```python
import jax
import jax.numpy as jnp
from jax import lax
from jax.sharding import PartitionSpec as P


def inner_gram(matrix):
    return lax.dot_general(
        matrix, matrix, (((0,), (0,)), ((), ())), preferred_element_type=jnp.float32
    )


def gram_solve(rhs, gram):
    lower_factor = jnp.linalg.cholesky(gram)
    return jax.scipy.linalg.cho_solve((lower_factor, True), rhs.T).T


def body(frames, row_factor, col_factor, row_history, col_history, time_gram):
    row_part = inner_gram(row_factor)
    col_part = inner_gram(col_factor)
    local_slab = jnp.einsum("bij,jr->bir", frames, col_factor, preferred_element_type=jnp.float32)
    slab_products, col_gram = lax.psum((local_slab, col_part), "col")
    rhs_part = jnp.sum(slab_products * row_factor.astype(jnp.float32)[None], axis=1)
    row_gram, frame_rhs = lax.psum((row_part, rhs_part), "row")
    frame_factor = gram_solve(frame_rhs, row_gram * col_gram)
    time_new = time_gram + jnp.dot(frame_factor.T, frame_factor, precision=lax.Precision.HIGHEST)
    row_sums = row_history + jnp.sum(frame_factor[:, None, :] * slab_products, axis=0)
    new_row = gram_solve(row_sums, time_new * col_gram).astype(jnp.bfloat16)
    new_gram_part = inner_gram(new_row)
    products = jnp.einsum("bij,ir->bjr", frames, new_row, preferred_element_type=jnp.float32)
    col_total, new_row_gram = lax.psum(
        (jnp.sum(frame_factor[:, None, :] * products, axis=0), new_gram_part), "row"
    )
    new_col = gram_solve(col_history + col_total, time_new * new_row_gram).astype(jnp.bfloat16)
    return (frame_factor, new_row, new_col)


def solution(mesh):
    in_specs = (
        P(None, "row", "col"),
        P("row", None),
        P("col", None),
        P("row", None),
        P("col", None),
        P(),
    )
    out_specs = (P(), P("row", None), P("col", None))
    return jax.shard_map(body, mesh=mesh, in_specs=in_specs, out_specs=out_specs, check_vma=False)
```

profile of v0, /device:TPU:0, one launch (start us, length us, event | category | flops | bytes accessed | tf_op | source)
XLA Modules:
  0.0 533.5 jit_solution(14045542823402398835)
XLA Ops:
  7.2 2.0 fusion.47
  9.3 2.8 fusion.3
  14.9 108.3 %all-reduce.7.cloned.1.call-done = f32[256,256]{0,1:T(8,128)} async-done(((f32[256,256]{0,1:T(8,128)}), f32[256,256]{0,1:T(8,128)}) %all-reduce.7.cloned.1.call-update) | async-done | bytes 262160 | tf_op jit(solution)/shard_map/psum | solution.py:24
  123.2 21.6 %all-reduce.11.cloned.1.call-done = (f32[256,256]{0,1:T(8,128)}, f32[4,256,256]{2,1,0:T(8,128)}) async-done(((f32[256,256]{0,1:T(8,128)}, f32[4,256,256]{2,1,0:T(8,128)}), (f32[256,256]{0,1:T(8,128)}, f32[4,256,256]{2,1,0:T(8,128)})) %all-reduce.11.cloned.1.call-update) | async-done | bytes 1310736 | tf_op jit(solution)/shard_map/psum | solution.py:22
  148.4 11.7 %cholesky.172 = f32[128,128]{1,0:T(8,128)S(1)} custom-call(f32[128,128]{1,0:T(8,128)S(1)} %cholesky.270), custom_call_target="Cholesky" | custom-call | tf_op jit(solution)/shard_map/jit(cholesky)/cholesky | solution.py:14
  160.2 9.8 %custom-call.34 = f32[1,128,128]{1,2,0:T(8,128)S(1)} custom-call(f32[1,128,128]{2,1,0:T(8,128)S(1)} %get-tuple-element.79), custom_call_target="InvertDiagBlocksLowerTriangular" | custom-call | tf_op jit(solution)/shard_map/jit(cholesky)/cholesky | solution.py:14
  172.2 11.7 %cholesky.189 = f32[128,128]{1,0:T(8,128)S(1)} custom-call(f32[128,128]{1,0:T(8,128)S(1)} %convolution_subtract_fusion.6), custom_call_target="Cholesky" | custom-call | tf_op jit(solution)/shard_map/jit(cholesky)/cholesky | solution.py:14
  186.9 4.3 while.3
  191.8 20.5 %custom-call.29 = f32[2,128,128]{1,2,0:T(8,128)S(1)} custom-call(f32[2,128,128]{2,1,0:T(8,128)} %copy-done.13), custom_call_target="InvertDiagBlocksLowerTriangular" | custom-call | tf_op jit(solution)/shard_map/jit(_cho_solve)/triangular_solve | solution.py:15
  213.3 42.0 %psum.45 = f32[256,4]{0,1:T(4,128)S(1)} all-reduce(f32[256,4]{0,1:T(4,128)S(1)} %bitcast.139), channel_id=1, replica_groups=mesh['row'=16,'col'=2] {'row'}, use_global_device_ids=true, to_apply=%region_8.10 | all-reduce | flops 1024 | bytes 8192 | tf_op jit(solution)/shard_map/psum | solution.py:24
  256.7 2.2 fusion.44
  261.4 11.7 %cholesky.206 = f32[128,128]{1,0:T(8,128)S(1)} custom-call(f32[128,128]{1,0:T(8,128)S(1)} %cholesky.273), custom_call_target="Cholesky" | custom-call | tf_op jit(solution)/shard_map/jit(cholesky)/cholesky | solution.py:14
  273.1 9.8 %custom-call.35 = f32[1,128,128]{1,2,0:T(8,128)S(1)} custom-call(f32[1,128,128]{2,1,0:T(8,128)S(1)} %get-tuple-element.75), custom_call_target="InvertDiagBlocksLowerTriangular" | custom-call | tf_op jit(solution)/shard_map/jit(cholesky)/cholesky | solution.py:14
  285.1 11.7 %cholesky.223 = f32[128,128]{1,0:T(8,128)S(1)} custom-call(f32[128,128]{1,0:T(8,128)S(1)} %convolution_subtract_fusion.5), custom_call_target="Cholesky" | custom-call | tf_op jit(solution)/shard_map/jit(cholesky)/cholesky | solution.py:14
  300.5 4.1 while.4
  305.3 29.2 %custom-call.30 = f32[2,128,128]{1,2,0:T(8,128)S(1)} custom-call(f32[2,128,128]{2,1,0:T(8,128)} %copy-done.14), custom_call_target="InvertDiagBlocksLowerTriangular" | custom-call | tf_op jit(solution)/shard_map/jit(_cho_solve)/triangular_solve | solution.py:15
  340.1 1.8 fusion
  341.9 1.6 copy.27
  344.2 108.3 %all-reduce.9.cloned.1.call-done = (f32[1024,256]{0,1:T(8,128)}, f32[256,256]{0,1:T(8,128)}) async-done(((f32[1024,256]{0,1:T(8,128)}, f32[256,256]{0,1:T(8,128)}), (f32[1024,256]{0,1:T(8,128)}, f32[256,256]{0,1:T(8,128)})) %all-reduce.9.cloned.1.call-update) | async-done | bytes 1310736 | tf_op jit(solution)/shard_map/psum | solution.py:31
  456.1 11.7 %cholesky.240 = f32[128,128]{1,0:T(8,128)S(1)} custom-call(f32[128,128]{1,0:T(8,128)S(1)} %cholesky.276), custom_call_target="Cholesky" | custom-call | tf_op jit(solution)/shard_map/jit(cholesky)/cholesky | solution.py:14
  467.9 9.8 %custom-call.36 = f32[1,128,128]{1,2,0:T(8,128)S(1)} custom-call(f32[1,128,128]{2,1,0:T(8,128)S(1)} %get-tuple-element.71), custom_call_target="InvertDiagBlocksLowerTriangular" | custom-call | tf_op jit(solution)/shard_map/jit(cholesky)/cholesky | solution.py:14
  479.9 11.9 %cholesky.257 = f32[128,128]{1,0:T(8,128)S(1)} custom-call(f32[128,128]{1,0:T(8,128)S(1)} %convolution_subtract_fusion.4), custom_call_target="Cholesky" | custom-call | tf_op jit(solution)/shard_map/jit(cholesky)/cholesky | solution.py:14
  495.4 4.1 while.5
  500.2 20.5 %custom-call.31 = f32[2,128,128]{1,2,0:T(8,128)S(1)} custom-call(f32[2,128,128]{2,1,0:T(8,128)} %copy-done.12), custom_call_target="InvertDiagBlocksLowerTriangular" | custom-call | tf_op jit(solution)/shard_map/jit(_cho_solve)/triangular_solve | solution.py:15
  (126 shorter events, 54.4 us)
Async XLA Ops:
  7.2 2.2 copy-start
  7.2 116.0 %all-reduce.7.cloned.1.call-start = ((), (), s32[]{:S(2)}) async-start(), calls=%async_computation | async-start | bytes 524288 | tf_op jit(solution)/shard_map/psum | solution.py:24
  9.3 2.9 copy-start.1
  9.3 135.5 %all-reduce.11.cloned.1.call-start = ((), (), s32[]{:S(2)}) async-start(), calls=%async_computation.2 | async-start | bytes 2621440 | tf_op jit(solution)/shard_map/psum | solution.py:22
  12.2 1.1 copy-start.3
  12.2 1.9 copy-start.11
  13.3 439.2 %all-reduce.9.cloned.1.call-start = ((), (), s32[]{:S(2)}) async-start(), calls=%async_computation.1 | async-start | bytes 2621440 | tf_op jit(solution)/shard_map/psum | solution.py:31
  145.9 66.4 %copy-start.2 = (f32[4,256,256]{2,1,0:T(8,128)S(1)}, f32[4,256,256]{2,1,0:T(8,128)}, u32[]{:S(2)}) copy-start(f32[4,256,256]{2,1,0:T(8,128)} %get-tuple-element.61) | copy-start | bytes 3145732
  147.7 0.7 copy-start.7
  183.9 1.9 copy-start.6
  191.1 0.7 copy-start.13
  256.6 83.5 %copy-start.15 = (f32[4,256]{1,0:T(4,128)}, f32[4,256]{1,0:T(4,128)S(1)}, u32[]{:S(2)}) copy-start(f32[4,256]{1,0:T(4,128)S(1)} %fusion.36) | copy-start | bytes 12292
  260.7 0.7 copy-start.8
  296.9 2.6 copy-start.4
  304.6 0.7 copy-start.14
  334.5 1.8 copy-start.10
  455.4 0.7 copy-start.9
  491.8 2.6 copy-start.5
  499.5 0.7 copy-start.12
Sparse Core Ops, SparseCore 0:
  13.8 109.3 all-reduce.6
  125.7 19.0 all-reduce.10
  342.0 110.4 all-reduce.8
where the time goes:
time: 539 us; the launch traced here: 534 us
  waiting for transfers between devices  238 us (44%)
  other arithmetic  186 us (35%)
  blocking collectives  42 us (8%)
  matrix products  25.7 us (5%)
  local copies, waits for them, and re-layouts  23 us (4%)
  between operations  18.2 us (3%)
    psum x1, waiting for transfers between devices, body(): row_gram, frame_rhs = lax.psum((row_part, rhs_part), 'row')  108 us
    psum x1, waiting for transfers between devices, body(): lax.psum((jnp.sum(frame_factor[:, None, :] * products, axis=0), new_gram_...  108 us
    another operation x20, other arithmetic, gram_solve(): lower_factor = jnp.linalg.cholesky(gram)  103 us
    another operation x7, other arithmetic, gram_solve(): return jax.scipy.linalg.cho_solve((lower_factor, True), rhs.T).T  73.2 us
    psum x1, blocking collectives, body(): row_gram, frame_rhs = lax.psum((row_part, rhs_part), 'row')  42 us
    psum x1, waiting for transfers between devices, body(): slab_products, col_gram = lax.psum((local_slab, col_part), 'col')  21.6 us
    another operation x18, local copies, waits for them, and re-layouts  12.1 us
  transfers between devices with their start and end apart: 3, of which 3 were waited for; matrix products, arithmetic and copies ran while one was open for 1% of the time, Pallas kernels for 0%

commit v1 on v0

v1 whole, which is shorter than its diff:
```python
import functools

import jax
import jax.numpy as jnp
from jax import lax
from jax.experimental import pallas as pl
from jax.experimental.pallas import tpu as pltpu
from jax.sharding import PartitionSpec as P

MESH = pl.DeviceIdType.MESH
HIGHEST = lax.Precision.HIGHEST
F32 = jnp.float32
PIV = 4


def dot(a, b, dims, precision=None):
    return lax.dot_general(a, b, (dims, ((), ())), precision=precision, preferred_element_type=F32)


def small_inverse(m):
    m = [list(row) for row in m]
    size = len(m)
    for k in range(size):
        p = 1.0 / m[k][k]
        row = [p if j == k else m[k][j] * p for j in range(size)]
        for i in range(size):
            if i != k:
                f = m[i][k]
                m[i] = [-(f * p) if j == k else m[i][j] - f * row[j] for j in range(size)]
        m[k] = row
    return m


def invert(a_ref):
    n = a_ref.shape[0]
    lane = lax.broadcasted_iota(jnp.int32, (1, n), 1)
    step = 64

    def group(g, carry):
        base = pl.multiple_of(g * 8, 8)
        for j in range(0, 8, PIV):
            last = j + PIV == 8
            tile = a_ref[pl.ds(base, 8), :]
            m = [[tile[j + a : j + a + 1, j + b : j + b + 1] for b in range(PIV)] for a in range(PIV)]
            mi = small_inverse(m)
            inside = (lane >= j) & (lane < j + PIV)
            rows = [
                jnp.where(lane == j + b, 1.0, jnp.where(inside, 0.0, tile[j + b : j + b + 1, :]))
                for b in range(PIV)
            ]
            w = [sum(mi[a][b] * rows[b] for b in range(PIV)) for a in range(PIV)]
            for r in range(0, n, step):
                x = a_ref[r : r + step, :]
                y = jnp.where(inside, 0.0, x)
                for a in range(PIV):
                    y = y - x[:, j + a : j + a + 1] * w[a]
                a_ref[r : r + step, :] = pltpu.roll(y, n - 8, 1) if last else y
            for a in range(PIV):
                a_ref[pl.ds(base + j + a, 1), :] = pltpu.roll(w[a], n - 8, 1) if last else w[a]
        return carry

    lax.fori_loop(0, n // 8, group, 0)


def kernel(nrow, ncol, frames, rf, cf, rhist, chist, tgram, o_f, o_row, o_col,
           slab, cgram, rpart, rrecv, rfull, rhs, gpart, grecv, gfull, ppart, precv, pfull,
           mat, tnew, total,
           slab_s, slab_r, cg_s, cg_r, rs_s, rs_r, ag_s, ag_r, rhs_s, rhs_r,
           gs_s, gs_r, ga_s, ga_r, ps_s, ps_r, pa_s, pa_r):
    row = lax.axis_index("row")
    col = lax.axis_index("col")
    nb = frames.shape[0]
    rank = rf.shape[1]
    ch = rank // nrow
    pch = cf.shape[0] // nrow

    def send_all(axis, me, count, src, dst, s_sem, r_sem):
        def one(d, carry):
            p = lax.rem(me + d, count)
            pltpu.make_async_remote_copy(
                src_ref=src(p), dst_ref=dst, send_sem=s_sem.at[p], recv_sem=r_sem.at[me],
                device_id={axis: p}, device_id_type=MESH,
            ).start()
            return carry
        lax.fori_loop(1, count, one, 0)

    def wait_all(axis, me, count, src, dst, s_sem, r_sem, recv):
        def one(d, carry):
            p = lax.rem(me + d, count)
            copy = pltpu.make_async_remote_copy(
                src_ref=src(p), dst_ref=dst(p), send_sem=s_sem.at[p], recv_sem=r_sem.at[p],
                device_id={axis: p}, device_id_type=MESH,
            )
            if recv:
                copy.wait_recv()
            else:
                copy.wait_send()
            return carry
        lax.fori_loop(1, count, one, 0)

    exchanges = {
        "slab": ("col", col, ncol, lambda p: slab.at[col], slab, slab_s, slab_r),
        "cgram": ("col", col, ncol, lambda p: cgram.at[col], cgram, cg_s, cg_r),
        "rs": ("row", row, nrow, lambda p: rpart.at[p], rrecv, rs_s, rs_r),
        "ag": ("row", row, nrow, lambda p: rfull.at[row], rfull, ag_s, ag_r),
        "rhs": ("row", row, nrow, lambda p: rhs.at[row], rhs, rhs_s, rhs_r),
        "gs": ("row", row, nrow, lambda p: gpart.at[p], grecv, gs_s, gs_r),
        "ga": ("row", row, nrow, lambda p: gfull.at[row], gfull, ga_s, ga_r),
        "ps": ("row", row, nrow, lambda p: ppart.at[p], precv, ps_s, ps_r),
        "pa": ("row", row, nrow, lambda p: pfull.at[row], pfull, pa_s, pa_r),
    }

    def send(name):
        axis, me, count, src, buf, s, r = exchanges[name]
        send_all(axis, me, count, src, buf.at[me], s, r)

    def wait(name, recv=True):
        axis, me, count, src, buf, s, r = exchanges[name]
        wait_all(axis, me, count, src, lambda p: buf.at[p], s, r, recv)

    barrier = pltpu.get_barrier_semaphore()

    def greet(axis, me, count):
        def one(d, carry):
            pl.semaphore_signal(
                barrier, inc=1, device_id={axis: lax.rem(me + d, count)}, device_id_type=MESH
            )
            return carry
        lax.fori_loop(1, count, one, 0)

    greet("row", row, nrow)
    greet("col", col, ncol)

    gram = dot(rf[...], rf[...], ((0,), (0,)))
    for i in range(nrow):
        rpart[i] = gram[i * ch : (i + 1) * ch]
    rrecv[row] = rpart[row]
    cgram[col] = dot(cf[...], cf[...], ((0,), (0,)))
    pl.semaphore_wait(barrier, nrow + ncol - 2)
    send("rs")
    send("cgram")

    def slab_one(b, carry):
        slab[col, b] = dot(frames[b], cf[...], ((1,), (0,)))
        return carry

    lax.fori_loop(0, nb, slab_one, 0)
    send("slab")

    wait("rs")
    rfull[row] = sum((rrecv[i] for i in range(1, nrow)), rrecv[0])
    send("ag")

    wait("slab")
    for b in range(nb):
        s = sum((slab[c, b] for c in range(1, ncol)), slab[0, b])
        total[b] = s
        rhs[row, b : b + 1, :] = jnp.sum(s * rf[...].astype(F32), axis=0, keepdims=True)
    rhs[row, nb:8, :] = jnp.zeros((8 - nb, rank), F32)
    send("rhs")

    wait("cgram")
    tnew[...] = sum((cgram[c] for c in range(1, ncol)), cgram[0])
    wait("ag")
    for i in range(nrow):
        mat[i * ch : (i + 1) * ch, :] = rfull[i] * tnew[i * ch : (i + 1) * ch, :]
    invert(mat)
    wait("rhs")
    right = sum((rhs[i] for i in range(1, nrow)), rhs[0])
    ff = dot(right, mat[...], ((1,), (0,)), HIGHEST)
    o_f[...] = ff[:nb]

    time_new = tgram[...] + dot(ff, ff, ((0,), (0,)), HIGHEST)
    mat[...] = time_new * tnew[...]
    tnew[...] = time_new
    invert(mat)
    sums = rhist[...]
    for b in range(nb):
        sums = sums + ff[b : b + 1, :] * total[b]
    new_row = dot(sums, mat[...], ((1,), (0,)), HIGHEST).astype(jnp.bfloat16)
    o_row[...] = new_row

    gram = dot(new_row, new_row, ((0,), (0,)))
    for i in range(nrow):
        gpart[i] = gram[i * ch : (i + 1) * ch]
    grecv[row] = gpart[row]
    send("gs")
    wide = 256
    for j in range(0, cf.shape[0], wide):
        acc = jnp.zeros((wide, rank), F32)
        for b in range(nb):
            acc = acc + ff[b : b + 1, :] * dot(
                frames[b, :, j : j + wide], new_row, ((0,), (0,))
            )
        acc = acc.astype(jnp.bfloat16)
        for i in range(wide // pch):
            ppart[j // pch + i] = acc[i * pch : (i + 1) * pch]
    wait("gs")
    gfull[row] = sum((grecv[i] for i in range(1, nrow)), grecv[0])
    send("ga")
    precv[row] = ppart[row]
    send("ps")
    wait("ga")
    for i in range(nrow):
        mat[i * ch : (i + 1) * ch, :] = gfull[i] * tnew[i * ch : (i + 1) * ch, :]
    invert(mat)
    wait("ps")
    own = chist[pl.ds(pl.multiple_of(row * pch, pch), pch), :]
    for i in range(nrow):
        own = own + precv[i].astype(F32)
    pfull[row] = dot(own, mat[...], ((1,), (0,)), HIGHEST).astype(jnp.bfloat16)
    send("pa")
    wait("pa")
    for i in range(nrow):
        o_col[i * pch : (i + 1) * pch, :] = pfull[i]

    for name in exchanges:
        wait(name, recv=False)


def body(nrow, ncol, frames, rf, cf, rhist, chist, tgram):
    nb, rows, cols = frames.shape
    rank = rf.shape[1]
    ch, pch = rank // nrow, cols // nrow
    vm = pltpu.VMEM
    bf = jnp.bfloat16
    dma = pltpu.SemaphoreType.DMA
    counts = [ncol, ncol] + [nrow] * 7
    sems = [dma((c,)) for c in counts for _ in range(2)]
    space = pl.BlockSpec(memory_space=vm)
    flops = 2 * (2 * nb * rows * cols * rank + cols * rank * rank + 8 * rank**3)
    return pl.pallas_call(
        functools.partial(kernel, nrow, ncol),
        out_shape=(
            jax.ShapeDtypeStruct((nb, rank), F32),
            jax.ShapeDtypeStruct((rows, rank), bf),
            jax.ShapeDtypeStruct((cols, rank), bf),
        ),
        in_specs=[space] * 6,
        out_specs=(space,) * 3,
        scratch_shapes=[
            vm((ncol, nb, rows, rank), F32),
            vm((ncol, rank, rank), F32),
            vm((nrow, ch, rank), F32),
            vm((nrow, ch, rank), F32),
            vm((nrow, ch, rank), F32),
            vm((nrow, 8, rank), F32),
            vm((nrow, ch, rank), F32),
            vm((nrow, ch, rank), F32),
            vm((nrow, ch, rank), F32),
            vm((nrow, pch, rank), bf),
            vm((nrow, pch, rank), bf),
            vm((nrow, pch, rank), bf),
            vm((rank, rank), F32),
            vm((rank, rank), F32),
            vm((nb, rows, rank), F32),
        ] + sems,
        compiler_params=pltpu.CompilerParams(
            collective_id=0, has_side_effects=True, vmem_limit_bytes=48 * 1024 * 1024
        ),
        cost_estimate=pl.CostEstimate(
            flops=flops, bytes_accessed=frames.size * 2 + 4 * cols * rank * 2, transcendentals=0
        ),
    )(frames, rf, cf, rhist, chist, tgram)


def solution(mesh):
    in_specs = (
        P(None, "row", "col"),
        P("row", None),
        P("col", None),
        P("row", None),
        P("col", None),
        P(),
    )
    out_specs = (P(), P("row", None), P("col", None))
    return jax.shard_map(
        functools.partial(body, mesh.shape["row"], mesh.shape["col"]),
        mesh=mesh, in_specs=in_specs, out_specs=out_specs, check_vma=False,
    )
```

time: 539 us -> 294 us (0.55)
  Pallas kernels: 0 us -> 284 us
  waiting for transfers between devices: 238 us -> 0 us
  other arithmetic: 186 us -> 0 us
  blocking collectives: 42 us -> 0 us
  matrix products: 25.7 us -> 0 us
  between operations: 18.2 us -> 0.65 us
  local copies, waits for them, and re-layouts: 23 us -> 8.69 us
    pallas_call x0 -> x1, Pallas kernels: none -> 284 us  [body(): pl.pallas_call(functools.partial(kernel, nrow, ncol), out_shape=(jax.Shap...]
    psum x3 -> x0, waiting for transfers between devices: 238 us -> none  [the longest x1 108 us: body(): row_gram, frame_rhs = lax.psum((row_part, rhs_part), 'row')]
    another operation x27 -> x0, other arithmetic: 177 us -> none  [the longest x20 103 us: gram_solve(): lower_factor = jnp.linalg.cholesky(gram)]
    psum x1 -> x0, blocking collectives: 42 us -> none  [body(): row_gram, frame_rhs = lax.psum((row_part, rhs_part), 'row')]
    another operation x24 -> x0, matrix products: 14.9 us -> none  [the longest x18 8.46 us: gram_solve(): return jax.scipy.linalg.cho_solve((lower_factor, True), rhs.T).T]
    another operation x25 -> x0, local copies, waits for them, and re-layouts: 12.2 us -> none
    dot_general x6 -> x0, matrix products: 10.8 us -> none  [the longest x3 4.03 us: inner_gram(): lax.dot_general(matrix, matrix, (((0,), (0,)), ((), ())), preferred_eleme...]
  transfers between devices with their start and end apart: 3 -> 0, of which waited for: 3 -> 0; matrix products, arithmetic and copies ran while one was open for 1% -> 0% of each run, Pallas kernels for 0% -> 0%
where the time goes in v1:
time: 294 us
  Pallas kernels  284 us (97%)
  local copies, waits for them, and re-layouts  8.69 us (3%)
    pallas_call x1, Pallas kernels, body(): pl.pallas_call(functools.partial(kernel, nrow, ncol), out_shape=(jax.Shap...  284 us
    unnamed x15, local copies, waits for them, and re-layouts  8.69 us

profile of v1, /device:TPU:0, one launch (start us, length us, event | category | flops | bytes accessed | tf_op | source)
XLA Modules:
  0.0 293.6 jit_solution(1289565714536879879)
XLA Ops:
  0.6 0.0 copy-start
  0.6 1.6 copy-done
  2.2 0.0 copy-start.1
  2.2 1.2 copy-done.1
  3.4 0.0 copy-start.2
  3.5 1.0 copy-done.2
  4.5 0.0 copy-start.3
  4.5 0.9 copy-done.3
  5.4 0.0 copy-start.4
  5.4 0.9 copy-done.4
  6.4 0.0 copy-start.5
  6.4 0.9 copy-done.5
  7.3 284.3 %shard_map.85 = (f32[4,256]{1,0:T(4,128)S(1)}, bf16[256,256]{1,0:T(8,128)(2,1)S(1)}, bf16[1024,256]{1,0:T(8,128)(2,1)S(1)}) custom-call(bf16[4,256,1024]{2,1,0:T(8,128)(2,1)S(1)} %copy-done, bf16[256,256]{1,0:T(8,128)(2,1)S(1)} %copy-done.5, bf16[1024,256]{1,0:T(8,128)(2,1)S(1)} %copy-done.2, f32[256,256]{1,0:T(8,128)S(1)} %copy-done.3, ...), custom_call_target="tpu_custom_call" | custom-call | flops 1476395008 | bytes 4194304 | tf_op jit(solution)/shard_map/pallas_call | solution.py:232
  291.6 0.6 copy.12
  292.2 0.7 copy.13
  292.8 0.8 copy.14
Async XLA Ops:
  0.6 1.6 copy-start
  2.2 1.2 copy-start.1
  3.4 1.0 copy-start.2
  4.5 0.9 copy-start.3
  5.4 0.9 copy-start.4
  6.4 0.9 copy-start.5

commit v2 on v1

--- a/solution.py
+++ b/solution.py
@@ -10,60 +10,80 @@
 MESH = pl.DeviceIdType.MESH
 HIGHEST = lax.Precision.HIGHEST
 F32 = jnp.float32
-PIV = 4
+PIV = 8
 
 
 def dot(a, b, dims, precision=None):
     return lax.dot_general(a, b, (dims, ((), ())), precision=precision, preferred_element_type=F32)
 
 
-def small_inverse(m):
-    m = [list(row) for row in m]
-    size = len(m)
-    for k in range(size):
-        p = 1.0 / m[k][k]
-        row = [p if j == k else m[k][j] * p for j in range(size)]
-        for i in range(size):
-            if i != k:
-                f = m[i][k]
-                m[i] = [-(f * p) if j == k else m[i][j] - f * row[j] for j in range(size)]
-        m[k] = row
-    return m
+def eliminate(tile, lane):
+    n = tile.shape[1]
+    wide = (PIV, 128)
+    sub = lax.broadcasted_iota(jnp.int32, wide, 0)
+    cols = [jnp.broadcast_to(tile[:, b : b + 1], wide) for b in range(PIV)]
+    for k in range(PIV):
+        row = [jnp.broadcast_to(c[k : k + 1, :], wide) for c in cols]
+        p = 1.0 / row[k]
+        ck = cols[k]
+        here = sub == k
+        for b in range(PIV):
+            if b == k:
+                cols[b] = jnp.where(here, p, -(ck * p))
+            else:
+                w = row[b] * p
+                cols[b] = jnp.where(here, w, cols[b] - ck * w)
+    unit = (lane == lax.broadcasted_iota(jnp.int32, (PIV, n), 0)).astype(F32)
+    tile = jnp.where(lane < PIV, unit, tile)
+    out = None
+    for b in range(PIV):
+        scale = jnp.concatenate([cols[b]] * (n // 128), axis=1)
+        term = scale * jnp.broadcast_to(tile[b : b + 1, :], (PIV, n))
+        out = term if out is None else out + term
+    return out
+
+
+def spread(w):
+    return [jnp.broadcast_to(w[a : a + 1, :], w.shape) for a in range(PIV)]
+
+
+def update(x, ws, lane):
+    y = jnp.where(lane < PIV, 0.0, x)
+    for a in range(PIV):
+        y = y - jnp.broadcast_to(x[:, a : a + 1], x.shape) * ws[a]
+    return pltpu.roll(y, x.shape[1] - PIV, 1)
 
 
 def invert(a_ref):
     n = a_ref.shape[0]
-    lane = lax.broadcasted_iota(jnp.int32, (1, n), 1)
-    step = 64
+    groups = n // PIV
+    lane = lax.broadcasted_iota(jnp.int32, (PIV, n), 1)
+
+    def rows(g):
+        return pl.ds(pl.multiple_of(g * PIV, PIV), PIV)
+
+    def bulk(g, w, ws):
+        for r in range(0, n, PIV):
+            a_ref[r : r + PIV, :] = update(a_ref[r : r + PIV, :], ws, lane)
+        a_ref[rows(g), :] = pltpu.roll(w, n - PIV, 1)
+
+    w = eliminate(a_ref[0:PIV, :], lane)
+    tile = update(a_ref[PIV : 2 * PIV, :], spread(w), lane)
 
     def group(g, carry):
-        base = pl.multiple_of(g * 8, 8)
-        for j in range(0, 8, PIV):
-            last = j + PIV == 8
-            tile = a_ref[pl.ds(base, 8), :]
-            m = [[tile[j + a : j + a + 1, j + b : j + b + 1] for b in range(PIV)] for a in range(PIV)]
-            mi = small_inverse(m)
-            inside = (lane >= j) & (lane < j + PIV)
-            rows = [
-                jnp.where(lane == j + b, 1.0, jnp.where(inside, 0.0, tile[j + b : j + b + 1, :]))
-                for b in range(PIV)
-            ]
-            w = [sum(mi[a][b] * rows[b] for b in range(PIV)) for a in range(PIV)]
-            for r in range(0, n, step):
-                x = a_ref[r : r + step, :]
-                y = jnp.where(inside, 0.0, x)
-                for a in range(PIV):
-                    y = y - x[:, j + a : j + a + 1] * w[a]
-                a_ref[r : r + step, :] = pltpu.roll(y, n - 8, 1) if last else y
-            for a in range(PIV):
-                a_ref[pl.ds(base + j + a, 1), :] = pltpu.roll(w[a], n - 8, 1) if last else w[a]
-        return carry
-
-    lax.fori_loop(0, n // 8, group, 0)
-
-
-def kernel(nrow, ncol, frames, rf, cf, rhist, chist, tgram, o_f, o_row, o_col,
-           slab, cgram, rpart, rrecv, rfull, rhs, gpart, grecv, gfull, ppart, precv, pfull,
+        w, tile = carry
+        ws = spread(w)
+        later = update(a_ref[rows(lax.rem(g + 1, groups)), :], ws, lane)
+        fresh = eliminate(tile, lane)
+        bulk(g - 1, w, ws)
+        return fresh, update(later, spread(fresh), lane)
+
+    w, _ = lax.fori_loop(1, groups, group, (w, tile))
+    bulk(groups - 1, w, spread(w))
+
+
+def kernel(nrow, ncol, frames_h, rf_h, cf_h, rhist_h, chist_h, tgram_h, o_f, o_row, o_col,
+           frames, rf, cf, rhist, chist, tgram, in_s, slab, cgram, rpart, rrecv, rfull, rhs, gpart, grecv, gfull, ppart, precv, pfull,
            mat, tnew, total,
            slab_s, slab_r, cg_s, cg_r, rs_s, rs_r, ag_s, ag_r, rhs_s, rhs_r,
            gs_s, gs_r, ga_s, ga_r, ps_s, ps_r, pa_s, pa_r):
@@ -128,13 +148,23 @@
             return carry
         lax.fori_loop(1, count, one, 0)
 
+    loads = [
+        pltpu.make_async_copy(src, dst, in_s.at[i])
+        for i, (src, dst) in enumerate(
+            [(rf_h, rf), (cf_h, cf), (frames_h, frames), (tgram_h, tgram), (rhist_h, rhist), (chist_h, chist)]
+        )
+    ]
+    for load in loads:
+        load.start()
     greet("row", row, nrow)
     greet("col", col, ncol)
+    loads[0].wait()
 
     gram = dot(rf[...], rf[...], ((0,), (0,)))
     for i in range(nrow):
         rpart[i] = gram[i * ch : (i + 1) * ch]
     rrecv[row] = rpart[row]
+    loads[1].wait()
     cgram[col] = dot(cf[...], cf[...], ((0,), (0,)))
     pl.semaphore_wait(barrier, nrow + ncol - 2)
     send("rs")
@@ -144,6 +174,7 @@
         slab[col, b] = dot(frames[b], cf[...], ((1,), (0,)))
         return carry
 
+    loads[2].wait()
     lax.fori_loop(0, nb, slab_one, 0)
     send("slab")
 
@@ -170,6 +201,8 @@
     ff = dot(right, mat[...], ((1,), (0,)), HIGHEST)
     o_f[...] = ff[:nb]
 
+    for load in loads[3:]:
+        load.wait()
     time_new = tgram[...] + dot(ff, ff, ((0,), (0,)), HIGHEST)
     mat[...] = time_new * tnew[...]
     tnew[...] = time_new
@@ -236,9 +269,10 @@
             jax.ShapeDtypeStruct((rows, rank), bf),
             jax.ShapeDtypeStruct((cols, rank), bf),
         ),
-        in_specs=[space] * 6,
+        in_specs=[pl.BlockSpec(memory_space=pltpu.HBM)] * 6,
         out_specs=(space,) * 3,
-        scratch_shapes=[
+        scratch_shapes=[vm(x.shape, x.dtype) for x in (frames, rf, cf, rhist, chist, tgram)] + [
+            dma((6,)),
             vm((ncol, nb, rows, rank), F32),
             vm((ncol, rank, rank), F32),
             vm((nrow, ch, rank), F32),

time: 294 us -> 305 us (1.037)
  Pallas kernels: 284 us -> 295 us
    pallas_call x1, Pallas kernels: 284 us -> 295 us  [body(): pl.pallas_call(functools.partial(kernel, nrow, ncol), out_shape=(jax.Shap...]
where the time goes in v2:
time: 305 us; the launch traced here: 304 us
  Pallas kernels  295 us (97%)
  local copies, waits for them, and re-layouts  8.69 us (3%)
    pallas_call x1, Pallas kernels, body(): pl.pallas_call(functools.partial(kernel, nrow, ncol), out_shape=(jax.Shap...  295 us
    unnamed x15, local copies, waits for them, and re-layouts  8.69 us

profile of v2, /device:TPU:0, one launch (start us, length us, event | category | flops | bytes accessed | tf_op | source)
XLA Modules:
  0.0 304.2 jit_solution(1477386831277197131)
XLA Ops:
  0.6 0.0 copy-start
  0.6 1.6 copy-done
  2.2 0.0 copy-start.1
  2.2 1.2 copy-done.1
  3.4 0.0 copy-start.2
  3.5 1.0 copy-done.2
  4.5 0.0 copy-start.3
  4.5 0.9 copy-done.3
  5.4 0.0 copy-start.4
  5.4 0.9 copy-done.4
  6.4 0.0 copy-start.5
  6.4 0.9 copy-done.5
  7.3 294.9 %shard_map.85 = (f32[4,256]{1,0:T(4,128)S(1)}, bf16[256,256]{1,0:T(8,128)(2,1)S(1)}, bf16[1024,256]{1,0:T(8,128)(2,1)S(1)}) custom-call(bf16[4,256,1024]{2,1,0:T(8,128)(2,1)S(1)} %copy-done, bf16[256,256]{1,0:T(8,128)(2,1)S(1)} %copy-done.5, bf16[1024,256]{1,0:T(8,128)(2,1)S(1)} %copy-done.2, f32[256,256]{1,0:T(8,128)S(1)} %copy-done.3, ...), custom_call_target="tpu_custom_call" | custom-call | flops 1476395008 | bytes 4194304 | tf_op jit(solution)/shard_map/pallas_call | solution.py:265
  302.2 0.6 copy.12
  302.8 0.7 copy.13
  303.4 0.8 copy.14
Async XLA Ops:
  0.6 1.6 copy-start
  2.2 1.2 copy-start.1
  3.4 1.0 copy-start.2
  4.5 0.9 copy-start.3
  5.4 0.9 copy-start.4
  6.4 0.9 copy-start.5

commit v3 on v0

v3 whole, which is shorter than its diff:
```python
import functools

import jax
import jax.numpy as jnp
from jax import lax
from jax.experimental import pallas as pl
from jax.experimental.pallas import tpu as pltpu
from jax.sharding import PartitionSpec as P

MESH = pl.DeviceIdType.MESH
HIGHEST = lax.Precision.HIGHEST
F32 = jnp.float32
PIV = 8


def dot(a, b, dims, precision=None):
    return lax.dot_general(a, b, (dims, ((), ())), precision=precision, preferred_element_type=F32)


def eliminate(tile, turned, g, lane):
    n = tile.shape[1]
    wide = (PIV, 128)
    sub = lax.broadcasted_iota(jnp.int32, wide, 0)
    cols = [jnp.broadcast_to(turned[:, b : b + 1], wide) for b in range(PIV)]
    for k in range(PIV):
        row = [jnp.broadcast_to(c[k : k + 1, :], wide) for c in cols]
        p = 1.0 / row[k]
        ck = cols[k]
        here = sub == k
        for b in range(PIV):
            if b == k:
                cols[b] = jnp.where(here, p, -(ck * p))
            else:
                w = row[b] * p
                cols[b] = jnp.where(here, w, cols[b] - ck * w)
    at = lane - g * PIV
    unit = (at == lax.broadcasted_iota(jnp.int32, (PIV, n), 0)).astype(F32)
    tile = jnp.where((at >= 0) & (at < PIV), unit, tile)
    out = None
    for b in range(PIV):
        scale = jnp.concatenate([cols[b]] * (n // 128), axis=1)
        term = scale * jnp.broadcast_to(tile[b : b + 1, :], (PIV, n))
        out = term if out is None else out + term
    return out


def invert(a_ref, w_ref):
    n = a_ref.shape[0]
    groups = n // PIV
    lane = lax.broadcasted_iota(jnp.int32, (PIV, n), 1)
    lanes = lax.broadcasted_iota(jnp.int32, (n, n), 1)

    def rows(g):
        return pl.ds(pl.multiple_of(g * PIV, PIV), PIV)

    def front(tile, g):
        return pltpu.roll(tile, lax.rem(n - g * PIV, n), 1)

    def update(tile, w, g):
        turned = front(tile, g)
        y = jnp.where((lane >= g * PIV) & (lane < g * PIV + PIV), 0.0, tile)
        for a in range(PIV):
            y = y - jnp.broadcast_to(turned[:, a : a + 1], y.shape) * jnp.broadcast_to(w[a : a + 1, :], y.shape)
        return y

    def bulk(g, w):
        w_ref[rows(g), :] = w
        inside = (lanes >= g * PIV) & (lanes < g * PIV + PIV)
        x = a_ref[...]
        w_all = w_ref[...]
        a_ref[...] = jnp.where(inside, 0.0, x) - dot(jnp.where(inside, x, 0.0), w_all, ((1,), (0,)), HIGHEST)
        a_ref[rows(g), :] = w
        w_ref[rows(g), :] = jnp.zeros_like(w)

    w_ref[...] = jnp.zeros_like(w_ref)
    w = eliminate(a_ref[0:PIV, :], front(a_ref[0:PIV, :], 0), 0, lane)
    tile = update(a_ref[PIV : 2 * PIV, :], w, 0)

    def group(g, carry):
        w, tile = carry
        later = update(a_ref[rows(lax.rem(g + 1, groups)), :], w, g - 1)
        fresh = eliminate(tile, front(tile, g), g, lane)
        bulk(g - 1, w)
        return fresh, update(later, fresh, g)

    w, _ = lax.fori_loop(1, groups, group, (w, tile))
    bulk(groups - 1, w)


def helpers(axis, count):
    me = lax.axis_index(axis)

    def each(fn):
        def one(d, carry):
            fn(lax.rem(me + d, count))
            return carry
        lax.fori_loop(1, count, one, 0)

    def copy(p, src, buf, sems, slot):
        return pltpu.make_async_remote_copy(
            src_ref=src, dst_ref=buf.at[slot], send_sem=sems[0].at[p], recv_sem=sems[1].at[slot],
            device_id={axis: p}, device_id_type=MESH,
        )

    def send(src, buf, sems):
        each(lambda p: copy(p, src(p), buf, sems, me).start())

    def wait(buf, sems):
        each(lambda p: copy(p, buf.at[p], buf, sems, p).wait_recv())

    def drain(src, buf, sems):
        each(lambda p: copy(p, src(p), buf, sems, me).wait_send())

    def greet():
        each(lambda p: pl.semaphore_signal(
            pltpu.get_barrier_semaphore(), inc=1, device_id={axis: p}, device_id_type=MESH))

    return me, send, wait, drain, greet


def total_of(ref):
    return sum((ref[i] for i in range(1, ref.shape[0])), ref[0])


def first(nrow, ncol, frames, rf, cf, o_gram, o_cgram, o_total, o_rhs,
          slab, cgram, rpart, rrecv, rfull, rhs, *sems):
    slab_m, cg_m, rs_m, ag_m, rhs_m = (sems[2 * i : 2 * i + 2] for i in range(5))
    row, send_r, wait_r, drain_r, greet_r = helpers("row", nrow)
    col, send_c, wait_c, drain_c, greet_c = helpers("col", ncol)
    nb = frames.shape[0]
    rank = rf.shape[1]
    ch = rank // nrow
    greet_r()
    greet_c()
    gram = dot(rf[...], rf[...], ((0,), (0,)))
    for i in range(nrow):
        rpart[i] = gram[i * ch : (i + 1) * ch]
    rrecv[row] = rpart[row]
    cgram[col] = dot(cf[...], cf[...], ((0,), (0,)))
    pl.semaphore_wait(pltpu.get_barrier_semaphore(), nrow + ncol - 2)
    send_r(lambda p: rpart.at[p], rrecv, rs_m)
    send_c(lambda p: cgram.at[col], cgram, cg_m)

    def slab_one(b, carry):
        slab[col, b] = dot(frames[b], cf[...], ((1,), (0,)))
        return carry

    lax.fori_loop(0, nb, slab_one, 0)
    send_c(lambda p: slab.at[col], slab, slab_m)
    wait_r(rrecv, rs_m)
    rfull[row] = total_of(rrecv)
    send_r(lambda p: rfull.at[row], rfull, ag_m)
    wait_c(slab, slab_m)
    for b in range(nb):
        s = sum((slab[c, b] for c in range(1, ncol)), slab[0, b])
        o_total[b] = s
        rhs[row, b : b + 1, :] = jnp.sum(s * rf[...].astype(F32), axis=0, keepdims=True)
    rhs[row, nb:8, :] = jnp.zeros((8 - nb, rank), F32)
    send_r(lambda p: rhs.at[row], rhs, rhs_m)
    wait_c(cgram, cg_m)
    o_cgram[...] = total_of(cgram)
    wait_r(rfull, ag_m)
    for i in range(nrow):
        o_gram[i * ch : (i + 1) * ch, :] = rfull[i] * o_cgram[i * ch : (i + 1) * ch, :]
    wait_r(rhs, rhs_m)
    o_rhs[...] = total_of(rhs)
    drain_r(lambda p: rpart.at[p], rrecv, rs_m)
    drain_c(lambda p: cgram.at[col], cgram, cg_m)
    drain_c(lambda p: slab.at[col], slab, slab_m)
    drain_r(lambda p: rfull.at[row], rfull, ag_m)
    drain_r(lambda p: rhs.at[row], rhs, rhs_m)


def second(nb, gram, cgram, rhs, tgram, o_f, o_ff, o_time, o_mat, mat, w):
    mat[...] = gram[...]
    invert(mat, w)
    ff = dot(rhs[...], mat[...], ((1,), (0,)), HIGHEST)
    o_ff[...] = ff
    o_f[...] = ff[:nb]
    time_new = tgram[...] + dot(ff, ff, ((0,), (0,)), HIGHEST)
    o_time[...] = time_new
    o_mat[...] = time_new * cgram[...]


def third(nb, gram, ff, total, rhist, o_row, mat, w):
    mat[...] = gram[...]
    invert(mat, w)
    sums = rhist[...]
    for b in range(nb):
        sums = sums + ff[b : b + 1, :] * total[b]
    o_row[...] = dot(sums, mat[...], ((1,), (0,)), HIGHEST).astype(jnp.bfloat16)


def fourth(nrow, frames, new_row, ff, tnew, chist, o_mat, o_sum,
           gpart, grecv, gfull, ppart, precv, *sems):
    gs_m, ga_m, ps_m = (sems[2 * i : 2 * i + 2] for i in range(3))
    row, send, wait, drain, greet = helpers("row", nrow)
    nb, _, cols = frames.shape
    rank = ff.shape[1]
    ch, pch = rank // nrow, cols // nrow
    greet()
    gram = dot(new_row[...], new_row[...], ((0,), (0,)))
    for i in range(nrow):
        gpart[i] = gram[i * ch : (i + 1) * ch]
    grecv[row] = gpart[row]
    pl.semaphore_wait(pltpu.get_barrier_semaphore(), nrow - 1)
    send(lambda p: gpart.at[p], grecv, gs_m)
    wide = 256
    for j in range(0, cols, wide):
        acc = jnp.zeros((wide, rank), F32)
        for b in range(nb):
            acc = acc + ff[b : b + 1, :] * dot(
                frames[b, :, j : j + wide], new_row[...], ((0,), (0,))
            )
        acc = acc.astype(jnp.bfloat16)
        for i in range(wide // pch):
            ppart[j // pch + i] = acc[i * pch : (i + 1) * pch]
    wait(grecv, gs_m)
    gfull[row] = total_of(grecv)
    send(lambda p: gfull.at[row], gfull, ga_m)
    precv[row] = ppart[row]
    send(lambda p: ppart.at[p], precv, ps_m)
    wait(gfull, ga_m)
    for i in range(nrow):
        o_mat[i * ch : (i + 1) * ch, :] = gfull[i] * tnew[i * ch : (i + 1) * ch, :]
    wait(precv, ps_m)
    own = chist[pl.ds(pl.multiple_of(row * pch, pch), pch), :]
    for i in range(nrow):
        own = own + precv[i].astype(F32)
    o_sum[...] = own
    drain(lambda p: gpart.at[p], grecv, gs_m)
    drain(lambda p: gfull.at[row], gfull, ga_m)
    drain(lambda p: ppart.at[p], precv, ps_m)


def fifth(gram, own, o_own, mat, w):
    mat[...] = gram[...]
    invert(mat, w)
    o_own[...] = dot(own[...], mat[...], ((1,), (0,)), HIGHEST).astype(jnp.bfloat16)


def sixth(nrow, own, o_col, pfull, *pa_m):
    row, send, wait, drain, greet = helpers("row", nrow)
    pch = own.shape[0]
    greet()
    pfull[row] = own[...]
    pl.semaphore_wait(pltpu.get_barrier_semaphore(), nrow - 1)
    send(lambda p: pfull.at[row], pfull, pa_m)
    wait(pfull, pa_m)
    for i in range(nrow):
        o_col[i * pch : (i + 1) * pch, :] = pfull[i]
    drain(lambda p: pfull.at[row], pfull, pa_m)


def body(nrow, ncol, frames, rf, cf, rhist, chist, tgram):
    nb, rows, cols = frames.shape
    rank = rf.shape[1]
    ch, pch = rank // nrow, cols // nrow
    vm = pltpu.VMEM
    bf = jnp.bfloat16
    space = pl.BlockSpec(memory_space=vm)
    shape = jax.ShapeDtypeStruct
    square = shape((rank, rank), F32)

    def sems(*counts):
        return [pltpu.SemaphoreType.DMA((c,)) for c in counts for _ in range(2)]

    def call(fn, name, outs, scratch, args, collective=None):
        remote = {} if collective is None else dict(collective_id=collective, has_side_effects=True)
        return pl.pallas_call(
            fn, out_shape=outs, in_specs=[space] * len(args), out_specs=(space,) * len(outs),
            scratch_shapes=scratch, name=name,
            compiler_params=pltpu.CompilerParams(vmem_limit_bytes=48 * 1024 * 1024, **remote),
        )(*args)

    block = vm((nrow, ch, rank), F32)
    gram, cgram, total, rhs = call(
        functools.partial(first, nrow, ncol), "first",
        (square, square, shape((nb, rows, rank), F32), shape((8, rank), F32)),
        [vm((ncol, nb, rows, rank), F32), vm((ncol, rank, rank), F32), block, block, block,
         vm((nrow, 8, rank), F32)] + sems(ncol, ncol, nrow, nrow, nrow),
        (frames, rf, cf), 0)
    local = [vm((rank, rank), F32)] * 2
    f, ff, tnew, mat = call(
        functools.partial(second, nb), "second",
        (shape((nb, rank), F32), shape((8, rank), F32), square, square), local, (gram, cgram, rhs, tgram))
    new_row, = call(
        functools.partial(third, nb), "third", (shape((rows, rank), bf),), local, (mat, ff, total, rhist))
    part = vm((nrow, pch, rank), bf)
    mat, own = call(
        functools.partial(fourth, nrow), "fourth", (square, shape((pch, rank), F32)),
        [block, block, block, part, part] + sems(nrow, nrow, nrow),
        (frames, new_row, ff, tnew, chist), 1)
    own, = call(fifth, "fifth", (shape((pch, rank), bf),), local, (mat, own))
    new_col, = call(
        functools.partial(sixth, nrow), "sixth", (shape((cols, rank), bf),), [part] + sems(nrow), (own,), 2)
    return f, new_row, new_col


def solution(mesh):
    in_specs = (
        P(None, "row", "col"),
        P("row", None),
        P("col", None),
        P("row", None),
        P("col", None),
        P(),
    )
    out_specs = (P(), P("row", None), P("col", None))
    return jax.shard_map(
        functools.partial(body, mesh.shape["row"], mesh.shape["col"]),
        mesh=mesh, in_specs=in_specs, out_specs=out_specs, check_vma=False,
    )
```

time: 539 us -> 120 us (0.22)
  waiting for transfers between devices: 238 us -> 0 us
  other arithmetic: 186 us -> 0 us
  Pallas kernels: 0 us -> 110 us
  blocking collectives: 42 us -> 0 us
  matrix products: 25.7 us -> 0 us
  between operations: 18.2 us -> 0.69 us
  local copies, waits for them, and re-layouts: 23 us -> 7.13 us
    psum x3 -> x0, waiting for transfers between devices: 238 us -> none  [the longest x1 108 us: body(): row_gram, frame_rhs = lax.psum((row_part, rhs_part), 'row')]
    another operation x27 -> x0, other arithmetic: 177 us -> none  [the longest x20 103 us: gram_solve(): lower_factor = jnp.linalg.cholesky(gram)]
    pallas_call x0 -> x6, Pallas kernels: none -> 110 us  [call(): pl.pallas_call(fn, out_shape=outs, in_specs=[space] * len(args), out_spec...]
    psum x1 -> x0, blocking collectives: 42 us -> none  [body(): row_gram, frame_rhs = lax.psum((row_part, rhs_part), 'row')]
    another operation x24 -> x0, matrix products: 14.9 us -> none  [the longest x18 8.46 us: gram_solve(): return jax.scipy.linalg.cho_solve((lower_factor, True), rhs.T).T]
    another operation x25 -> x0, local copies, waits for them, and re-layouts: 12.2 us -> none
    dot_general x6 -> x0, matrix products: 10.8 us -> none  [the longest x3 4.03 us: inner_gram(): lax.dot_general(matrix, matrix, (((0,), (0,)), ((), ())), preferred_eleme...]
  transfers between devices with their start and end apart: 3 -> 0, of which waited for: 3 -> 0; matrix products, arithmetic and copies ran while one was open for 1% -> 0% of each run, Pallas kernels for 0% -> 0%
where the time goes in v3:
time: 120 us; the launch traced here: 118 us
  Pallas kernels  110 us (92%)
  local copies, waits for them, and re-layouts  7.13 us (6%)
    pallas_call x6, Pallas kernels, call(): pl.pallas_call(fn, out_shape=outs, in_specs=[space] * len(args), out_spec...  110 us
    unnamed x17, local copies, waits for them, and re-layouts  7.13 us

profile of v3, /device:TPU:0, one launch (start us, length us, event | category | flops | bytes accessed | tf_op | source)
XLA Modules:
  0.0 118.0 jit_solution(16139198077022441040)
XLA Ops:
  0.6 0.0 copy-start
  0.6 1.6 %copy-done = bf16[4,256,1024]{2,1,0:T(8,128)(2,1)S(1)} copy-done((bf16[4,256,1024]{2,1,0:T(8,128)(2,1)S(1)}, bf16[4,256,1024]{2,1,0:T(8,128)(2,1)}, u32[]{:S(2)}) %copy-start) | copy-done | bytes 2097176
  2.2 0.0 copy-start.4
  2.2 1.0 copy-done.4
  3.3 0.0 copy-start.7
  3.3 0.9 copy-done.7
  4.2 0.0 copy-start.1
  4.2 0.0 copy-start.2
  4.2 23.6 %first.1 = (f32[256,256]{1,0:T(8,128)S(1)}, f32[256,256]{1,0:T(8,128)S(1)}, f32[4,256,256]{2,1,0:T(8,128)S(1)}, f32[8,256]{1,0:T(8,128)S(1)}) custom-call(bf16[4,256,1024]{2,1,0:T(8,128)(2,1)S(1)} %copy-done, bf16[256,256]{1,0:T(8,128)(2,1)S(1)} %copy-done.7, bf16[1024,256]{1,0:T(8,128)(2,1)S(1)} %copy-done.4), custom_call_target="tpu_custom_call" | custom-call | tf_op jit(solution)/shard_map/first/pallas_call | solution.py:270
  27.8 0.0 copy-start.5
  27.8 0.9 copy-done.5
  28.7 14.3 %second.1 = (f32[4,256]{1,0:T(4,128)}, f32[8,256]{1,0:T(8,128)S(1)}, f32[256,256]{1,0:T(8,128)S(1)}, f32[256,256]{1,0:T(8,128)S(1)}) custom-call(f32[256,256]{1,0:T(8,128)S(1)} %get-tuple-element.13.gram, f32[256,256]{1,0:T(8,128)S(1)} %get-tuple-element.14.cgram, f32[8,256]{1,0:T(8,128)S(1)} %get-tuple-element.15.rhs, f32[256,256]{1,0:T(8,128)S(1)} %copy-done.5), custom_call_target="tpu_custom_call" | custom-call | tf_op jit(solution)/shard_map/second/pallas_call | solution.py:270
  43.0 0.0 copy-start.6
  43.0 0.9 copy-done.6
  44.0 14.6 %third.1.new_row = bf16[256,256]{1,0:T(8,128)(2,1)} custom-call(f32[256,256]{1,0:T(8,128)S(1)} %get-tuple-element.17.gram, f32[8,256]{1,0:T(8,128)S(1)} %get-tuple-element.18.ff, f32[4,256,256]{2,1,0:T(8,128)S(1)} %get-tuple-element.19.total, f32[256,256]{1,0:T(8,128)S(1)} %copy-done.6), custom_call_target="tpu_custom_call" | custom-call | tf_op jit(solution)/shard_map/third/pallas_call | solution.py:270
  58.6 0.0 copy-done.1
  58.6 0.0 copy-done.2
  58.6 0.0 copy-start.3
  58.6 0.9 copy-done.3
  59.5 28.2 %fourth.1 = (f32[256,256]{1,0:T(8,128)S(1)}, f32[64,256]{1,0:T(8,128)S(1)}) custom-call(bf16[4,256,1024]{2,1,0:T(8,128)(2,1)S(1)} %copy-done.1, bf16[256,256]{1,0:T(8,128)(2,1)S(1)} %copy-done.3, f32[8,256]{1,0:T(8,128)S(1)} %get-tuple-element.18.ff, f32[256,256]{1,0:T(8,128)S(1)} %get-tuple-element.20.tnew, f32[1024,256]{1,0:T(8,128)S(1)} %copy-done.2), custom_call_target="tpu_custom_call" | custom-call | tf_op jit(solution)/shard_map/fourth/pallas_call | solution.py:270
  87.7 13.6 %fifth.1.own = bf16[64,256]{1,0:T(8,128)(2,1)S(1)} custom-call(f32[256,256]{1,0:T(8,128)S(1)} %get-tuple-element.21.gram, f32[64,256]{1,0:T(8,128)S(1)} %get-tuple-element.22.own), custom_call_target="tpu_custom_call" | custom-call | tf_op jit(solution)/shard_map/fifth/pallas_call | solution.py:270
  101.3 15.9 %sixth.1 = bf16[1024,256]{1,0:T(8,128)(2,1)S(1)} custom-call(bf16[64,256]{1,0:T(8,128)(2,1)S(1)} %fifth.1.own), custom_call_target="tpu_custom_call" | custom-call | tf_op jit(solution)/shard_map/sixth/pallas_call | solution.py:270
  117.2 0.8 copy.10
Async XLA Ops:
  0.6 1.6 %copy-start = (bf16[4,256,1024]{2,1,0:T(8,128)(2,1)S(1)}, bf16[4,256,1024]{2,1,0:T(8,128)(2,1)}, u32[]{:S(2)}) copy-start(bf16[4,256,1024]{2,1,0:T(8,128)(2,1)} %frames.3) | copy-start | bytes 6291460
  2.2 1.0 copy-start.4
  3.3 0.9 copy-start.7
  4.2 54.4 %copy-start.1 = (bf16[4,256,1024]{2,1,0:T(8,128)(2,1)S(1)}, bf16[4,256,1024]{2,1,0:T(8,128)(2,1)}, u32[]{:S(2)}) copy-start(bf16[4,256,1024]{2,1,0:T(8,128)(2,1)} %frames.3) | copy-start | bytes 6291460
  4.2 54.4 %copy-start.2 = (f32[1024,256]{1,0:T(8,128)S(1)}, f32[1024,256]{1,0:T(8,128)}, u32[]{:S(2)}) copy-start(f32[1024,256]{1,0:T(8,128)} %chist.1) | copy-start | bytes 3145732
  27.8 1.0 copy-start.5
  43.0 0.9 copy-start.6
  58.6 0.9 copy-start.3

commit v4 on v3

v4 whole, which is shorter than its diff:
```python
import functools

import jax
import jax.numpy as jnp
from jax import lax
from jax.experimental import pallas as pl
from jax.experimental.pallas import tpu as pltpu
from jax.sharding import PartitionSpec as P

MESH = pl.DeviceIdType.MESH
HIGHEST = lax.Precision.HIGHEST
F32 = jnp.float32
PIV = 8


def dot(a, b, dims, precision=None):
    return lax.dot_general(a, b, (dims, ((), ())), precision=precision, preferred_element_type=F32)


def eliminate(tile, turned, g, lane):
    n = tile.shape[1]
    wide = (PIV, 128)
    sub = lax.broadcasted_iota(jnp.int32, wide, 0)
    cols = [jnp.broadcast_to(turned[:, b : b + 1], wide) for b in range(PIV)]
    for k in range(PIV):
        row = [jnp.broadcast_to(c[k : k + 1, :], wide) for c in cols]
        p = 1.0 / row[k]
        ck = cols[k]
        here = sub == k
        for b in range(PIV):
            if b == k:
                cols[b] = jnp.where(here, p, -(ck * p))
            else:
                w = row[b] * p
                cols[b] = jnp.where(here, w, cols[b] - ck * w)
    at = lane - g * PIV
    unit = (at == lax.broadcasted_iota(jnp.int32, (PIV, n), 0)).astype(F32)
    tile = jnp.where((at >= 0) & (at < PIV), unit, tile)
    out = None
    for b in range(PIV):
        scale = jnp.concatenate([cols[b]] * (n // 128), axis=1)
        term = scale * jnp.broadcast_to(tile[b : b + 1, :], (PIV, n))
        out = term if out is None else out + term
    return out


def invert(a_ref, w_ref):
    n = a_ref.shape[0]
    groups = n // PIV
    lane = lax.broadcasted_iota(jnp.int32, (PIV, n), 1)
    lanes = lax.broadcasted_iota(jnp.int32, (n, n), 1)

    def rows(g):
        return pl.ds(pl.multiple_of(g * PIV, PIV), PIV)

    def front(tile, g):
        return pltpu.roll(tile, lax.rem(n - g * PIV, n), 1)

    def update(tile, w, g):
        turned = front(tile, g)
        y = jnp.where((lane >= g * PIV) & (lane < g * PIV + PIV), 0.0, tile)
        for a in range(PIV):
            y = y - jnp.broadcast_to(turned[:, a : a + 1], y.shape) * jnp.broadcast_to(w[a : a + 1, :], y.shape)
        return y

    def bulk(g, w):
        w_ref[rows(g), :] = w
        inside = (lanes >= g * PIV) & (lanes < g * PIV + PIV)
        x = a_ref[...]
        w_all = w_ref[...]
        a_ref[...] = jnp.where(inside, 0.0, x) - dot(jnp.where(inside, x, 0.0), w_all, ((1,), (0,)), HIGHEST)
        a_ref[rows(g), :] = w
        w_ref[rows(g), :] = jnp.zeros_like(w)

    w_ref[...] = jnp.zeros_like(w_ref)
    w = eliminate(a_ref[0:PIV, :], front(a_ref[0:PIV, :], 0), 0, lane)
    tile = update(a_ref[PIV : 2 * PIV, :], w, 0)

    def group(g, carry):
        w, tile = carry
        later = update(a_ref[rows(lax.rem(g + 1, groups)), :], w, g - 1)
        fresh = eliminate(tile, front(tile, g), g, lane)
        bulk(g - 1, w)
        return fresh, update(later, fresh, g)

    w, _ = lax.fori_loop(1, groups, group, (w, tile))
    bulk(groups - 1, w)


def helpers(axis, count):
    me = lax.axis_index(axis)

    def each(fn):
        def one(d, carry):
            fn(lax.rem(me + d, count))
            return carry
        lax.fori_loop(1, count, one, 0)

    def copy(p, src, buf, sems, slot):
        return pltpu.make_async_remote_copy(
            src_ref=src, dst_ref=buf.at[slot], send_sem=sems[0].at[p], recv_sem=sems[1].at[slot],
            device_id={axis: p}, device_id_type=MESH,
        )

    def send(src, buf, sems):
        each(lambda p: copy(p, src(p), buf, sems, me).start())

    def wait(buf, sems):
        each(lambda p: copy(p, buf.at[p], buf, sems, p).wait_recv())

    def drain(src, buf, sems):
        each(lambda p: copy(p, src(p), buf, sems, me).wait_send())

    def greet():
        each(lambda p: pl.semaphore_signal(
            pltpu.get_barrier_semaphore(), inc=1, device_id={axis: p}, device_id_type=MESH))

    return me, send, wait, drain, greet


def total_of(ref):
    return sum((ref[i] for i in range(1, ref.shape[0])), ref[0])


def kernel(nrow, ncol, share, frames, rf, cf, rhist, chist, tgram, o_f, o_row, o_col,
           slab, cgram, gall, recv, full, hall, hrecv, hfull, rhs, ppart, precv, pfull,
           total, mat, w, tnew, *sems):
    (slab_m, cg_m, rs_m, ag_m, ax_m, rhs_m, gs_m, ga_m, gx_m, ps_m, pa_m) = (
        sems[2 * i : 2 * i + 2] for i in range(11)
    )
    row, send_r, wait_r, drain_r, greet_r = helpers("row", nrow)
    col, send_c, wait_c, drain_c, greet_c = helpers("col", ncol)
    nb, _, cols = frames.shape
    rank = rf.shape[1]
    ch, pch = rank // nrow // share, cols // nrow
    mine = col if share > 1 else 0

    def gram_start(x, everything, got):
        gram = dot(x, x, ((0,), (0,)))
        for i in range(nrow * share):
            everything[i] = gram[i * ch : (i + 1) * ch]
        got[row] = everything[mine * nrow + row]

    def gram_scatter(everything, got, m):
        send_r(lambda p: everything.at[mine * nrow + p], got, m)

    def gram_gather(got, whole, m_in, m_out):
        wait_r(got, m_in)
        whole[mine, row] = total_of(got)
        send_r(lambda p: whole.at[mine, row], whole.at[mine], m_out)

    def gram_times(whole, other, m_in, m_x):
        wait_r(whole.at[mine], m_in)
        if share > 1:
            send_c(lambda p: whole.at[col], whole, m_x)
            wait_c(whole, m_x)
        for c in range(share):
            for i in range(nrow):
                at = (c * nrow + i) * ch
                mat[at : at + ch, :] = whole[c, i] * other[at : at + ch, :]

    def gram_drain(everything, got, whole, m_s, m_a, m_x):
        drain_r(lambda p: everything.at[mine * nrow + p], got, m_s)
        drain_r(lambda p: whole.at[mine, row], whole.at[mine], m_a)
        if share > 1:
            drain_c(lambda p: whole.at[col], whole, m_x)

    greet_r()
    greet_c()
    gram_start(rf[...], gall, recv)
    cgram[col] = dot(cf[...], cf[...], ((0,), (0,)))
    pl.semaphore_wait(pltpu.get_barrier_semaphore(), nrow + ncol - 2)
    gram_scatter(gall, recv, rs_m)
    send_c(lambda p: cgram.at[col], cgram, cg_m)

    def slab_one(b, carry):
        slab[col, b] = dot(frames[b], cf[...], ((1,), (0,)))
        return carry

    lax.fori_loop(0, nb, slab_one, 0)
    gram_gather(recv, full, rs_m, ag_m)
    send_c(lambda p: slab.at[col], slab, slab_m)
    wait_c(cgram, cg_m)
    tnew[...] = total_of(cgram)
    wait_c(slab, slab_m)
    for b in range(nb):
        s = sum((slab[c, b] for c in range(1, ncol)), slab[0, b])
        total[b] = s
        rhs[row, b : b + 1, :] = jnp.sum(s * rf[...].astype(F32), axis=0, keepdims=True)
    rhs[row, nb:8, :] = jnp.zeros((8 - nb, rank), F32)
    gram_times(full, tnew, ag_m, ax_m)
    send_r(lambda p: rhs.at[row], rhs, rhs_m)
    invert(mat, w)
    wait_r(rhs, rhs_m)
    ff = dot(total_of(rhs), mat[...], ((1,), (0,)), HIGHEST)
    o_f[...] = ff[:nb]

    time_new = tgram[...] + dot(ff, ff, ((0,), (0,)), HIGHEST)
    mat[...] = time_new * tnew[...]
    tnew[...] = time_new
    invert(mat, w)
    sums = rhist[...]
    for b in range(nb):
        sums = sums + ff[b : b + 1, :] * total[b]
    new_row = dot(sums, mat[...], ((1,), (0,)), HIGHEST).astype(jnp.bfloat16)
    o_row[...] = new_row

    gram_start(new_row, hall, hrecv)
    gram_scatter(hall, hrecv, gs_m)
    wide = 256

    def products(j):
        acc = jnp.zeros((wide, rank), F32)
        for b in range(nb):
            acc = acc + ff[b : b + 1, :] * dot(frames[b, :, j : j + wide], new_row, ((0,), (0,)))
        acc = acc.astype(jnp.bfloat16)
        for i in range(wide // pch):
            ppart[j // pch + i] = acc[i * pch : (i + 1) * pch]

    half = cols // 2
    for j in range(0, half, wide):
        products(j)
    gram_gather(hrecv, hfull, gs_m, ga_m)
    for j in range(half, cols, wide):
        products(j)
    gram_times(hfull, tnew, ga_m, gx_m)
    precv[row] = ppart[row]
    send_r(lambda p: ppart.at[p], precv, ps_m)
    invert(mat, w)
    wait_r(precv, ps_m)
    own = chist[pl.ds(pl.multiple_of(row * pch, pch), pch), :]
    for i in range(nrow):
        own = own + precv[i].astype(F32)
    pfull[row] = dot(own, mat[...], ((1,), (0,)), HIGHEST).astype(jnp.bfloat16)
    send_r(lambda p: pfull.at[row], pfull, pa_m)

    drain_c(lambda p: cgram.at[col], cgram, cg_m)
    drain_c(lambda p: slab.at[col], slab, slab_m)
    gram_drain(gall, recv, full, rs_m, ag_m, ax_m)
    drain_r(lambda p: rhs.at[row], rhs, rhs_m)
    gram_drain(hall, hrecv, hfull, gs_m, ga_m, gx_m)
    drain_r(lambda p: ppart.at[p], precv, ps_m)
    wait_r(pfull, pa_m)
    for i in range(nrow):
        o_col[i * pch : (i + 1) * pch, :] = pfull[i]
    drain_r(lambda p: pfull.at[row], pfull, pa_m)


def body(nrow, ncol, frames, rf, cf, rhist, chist, tgram):
    nb, rows, cols = frames.shape
    rank = rf.shape[1]
    share = ncol if rank % (8 * nrow * ncol) == 0 else 1
    ch, pch = rank // nrow // share, cols // nrow
    vm = pltpu.VMEM
    bf = jnp.bfloat16
    space = pl.BlockSpec(memory_space=vm)
    shape = jax.ShapeDtypeStruct
    counts = [ncol, ncol, nrow, nrow, ncol, nrow, nrow, nrow, ncol, nrow, nrow]
    square = vm((rank, rank), F32)
    part = vm((nrow, pch, rank), bf)
    gram = [
        vm((nrow * share, ch, rank), F32),
        vm((nrow, ch, rank), F32),
        vm((share, nrow, ch, rank), F32),
    ]
    return pl.pallas_call(
        functools.partial(kernel, nrow, ncol, share),
        out_shape=(shape((nb, rank), F32), shape((rows, rank), bf), shape((cols, rank), bf)),
        in_specs=[space] * 6,
        out_specs=(space,) * 3,
        scratch_shapes=[
            vm((ncol, nb, rows, rank), F32), vm((ncol, rank, rank), F32), *gram, *gram,
            vm((nrow, 8, rank), F32), part, part, part,
            vm((nb, rows, rank), F32), square, square, square,
        ] + [pltpu.SemaphoreType.DMA((c,)) for c in counts for _ in range(2)],
        compiler_params=pltpu.CompilerParams(
            collective_id=0, has_side_effects=True, vmem_limit_bytes=48 * 1024 * 1024
        ),
    )(frames, rf, cf, rhist, chist, tgram)


def solution(mesh):
    in_specs = (
        P(None, "row", "col"),
        P("row", None),
        P("col", None),
        P("row", None),
        P("col", None),
        P(),
    )
    out_specs = (P(), P("row", None), P("col", None))
    return jax.shard_map(
        functools.partial(body, mesh.shape["row"], mesh.shape["col"]),
        mesh=mesh, in_specs=in_specs, out_specs=out_specs, check_vma=False,
    )
```

time: 120 us -> 95.3 us (0.79)
  the two profiles are of different devices: /device:TPU:0 before, /device:TPU:15 now
where the time goes in v4:
time: 95.3 us; the launch traced here: 95 us
  Pallas kernels  85.7 us (90%)
  local copies, waits for them, and re-layouts  8.69 us (9%)
    pallas_call x1, Pallas kernels, body(): pl.pallas_call(functools.partial(kernel, nrow, ncol, share), out_shape=(s...  85.7 us
    unnamed x15, local copies, waits for them, and re-layouts  8.69 us

profile of v4, /device:TPU:15, one launch (start us, length us, event | category | flops | bytes accessed | tf_op | source)
XLA Modules:
  0.0 95.0 jit_solution(4074036145580603706)
XLA Ops:
  0.6 0.0 copy-start
  0.6 1.6 %copy-done = bf16[4,256,1024]{2,1,0:T(8,128)(2,1)S(1)} copy-done((bf16[4,256,1024]{2,1,0:T(8,128)(2,1)S(1)}, bf16[4,256,1024]{2,1,0:T(8,128)(2,1)}, u32[]{:S(2)}) %copy-start) | copy-done | bytes 2097176
  2.2 0.0 copy-start.1
  2.2 1.2 %copy-done.1 = f32[1024,256]{1,0:T(8,128)S(1)} copy-done((f32[1024,256]{1,0:T(8,128)S(1)}, f32[1024,256]{1,0:T(8,128)}, u32[]{:S(2)}) %copy-start.1) | copy-done | bytes 1048600
  3.4 0.0 copy-start.2
  3.5 1.0 %copy-done.2 = bf16[1024,256]{1,0:T(8,128)(2,1)S(1)} copy-done((bf16[1024,256]{1,0:T(8,128)(2,1)S(1)}, bf16[1024,256]{1,0:T(8,128)(2,1)}, u32[]{:S(2)}) %copy-start.2) | copy-done | bytes 524312
  4.5 0.0 copy-start.3
  4.5 0.9 copy-done.3
  5.4 0.0 copy-start.4
  5.4 0.9 copy-done.4
  6.4 0.0 copy-start.5
  6.4 0.9 copy-done.5
  7.3 85.7 %shard_map.85 = (f32[4,256]{1,0:T(4,128)S(1)}, bf16[256,256]{1,0:T(8,128)(2,1)S(1)}, bf16[1024,256]{1,0:T(8,128)(2,1)S(1)}) custom-call(bf16[4,256,1024]{2,1,0:T(8,128)(2,1)S(1)} %copy-done, bf16[256,256]{1,0:T(8,128)(2,1)S(1)} %copy-done.5, bf16[1024,256]{1,0:T(8,128)(2,1)S(1)} %copy-done.2, f32[256,256]{1,0:T(8,128)S(1)} %copy-done.3, ...), custom_call_target="tpu_custom_call" | custom-call | tf_op jit(solution)/shard_map/pallas_call | solution.py:266
  93.0 0.6 copy.12
  93.6 0.7 copy.13
  94.2 0.8 copy.14
Async XLA Ops:
  0.6 1.6 %copy-start = (bf16[4,256,1024]{2,1,0:T(8,128)(2,1)S(1)}, bf16[4,256,1024]{2,1,0:T(8,128)(2,1)}, u32[]{:S(2)}) copy-start(bf16[4,256,1024]{2,1,0:T(8,128)(2,1)} %frames.1) | copy-start | bytes 6291460
  2.2 1.2 %copy-start.1 = (f32[1024,256]{1,0:T(8,128)S(1)}, f32[1024,256]{1,0:T(8,128)}, u32[]{:S(2)}) copy-start(f32[1024,256]{1,0:T(8,128)} %chist.1) | copy-start | bytes 3145732
  3.4 1.0 %copy-start.2 = (bf16[1024,256]{1,0:T(8,128)(2,1)S(1)}, bf16[1024,256]{1,0:T(8,128)(2,1)}, u32[]{:S(2)}) copy-start(bf16[1024,256]{1,0:T(8,128)(2,1)} %cf.1) | copy-start | bytes 1572868
  4.5 0.9 copy-start.3
  5.4 0.9 copy-start.4
  6.4 0.9 copy-start.5

commit v5 on v4

--- a/solution.py
+++ b/solution.py
@@ -17,31 +17,27 @@
     return lax.dot_general(a, b, (dims, ((), ())), precision=precision, preferred_element_type=F32)
 
 
-def eliminate(tile, turned, g, lane):
-    n = tile.shape[1]
-    wide = (PIV, 128)
-    sub = lax.broadcasted_iota(jnp.int32, wide, 0)
-    cols = [jnp.broadcast_to(turned[:, b : b + 1], wide) for b in range(PIV)]
+def eliminate(cols):
+    cols = list(cols)
+    sub = lax.broadcasted_iota(jnp.int32, cols[0].shape, 0)
     for k in range(PIV):
-        row = [jnp.broadcast_to(c[k : k + 1, :], wide) for c in cols]
+        row = [jnp.broadcast_to(c[k : k + 1, :], c.shape) for c in cols]
         p = 1.0 / row[k]
         ck = cols[k]
         here = sub == k
-        for b in range(PIV):
+        for b in range(len(cols)):
             if b == k:
                 cols[b] = jnp.where(here, p, -(ck * p))
             else:
                 w = row[b] * p
                 cols[b] = jnp.where(here, w, cols[b] - ck * w)
-    at = lane - g * PIV
-    unit = (at == lax.broadcasted_iota(jnp.int32, (PIV, n), 0)).astype(F32)
-    tile = jnp.where((at >= 0) & (at < PIV), unit, tile)
-    out = None
-    for b in range(PIV):
-        scale = jnp.concatenate([cols[b]] * (n // 128), axis=1)
-        term = scale * jnp.broadcast_to(tile[b : b + 1, :], (PIV, n))
-        out = term if out is None else out + term
-    return out
+    return cols
+
+
+def add_up(terms):
+    while len(terms) > 1:
+        terms = [sum(terms[i : i + 2][1:], terms[i]) for i in range(0, len(terms), 2)]
+    return terms[0]
 
 
 def invert(a_ref, w_ref):
@@ -53,38 +49,77 @@
     def rows(g):
         return pl.ds(pl.multiple_of(g * PIV, PIV), PIV)
 
-    def front(tile, g):
-        return pltpu.roll(tile, lax.rem(n - g * PIV, n), 1)
-
-    def update(tile, w, g):
-        turned = front(tile, g)
-        y = jnp.where((lane >= g * PIV) & (lane < g * PIV + PIV), 0.0, tile)
-        for a in range(PIV):
-            y = y - jnp.broadcast_to(turned[:, a : a + 1], y.shape) * jnp.broadcast_to(w[a : a + 1, :], y.shape)
-        return y
+    def columns(tile, g):
+        turned = pltpu.roll(tile, lax.rem(2 * n - g * PIV, n), 1)
+        return [jnp.broadcast_to(turned[:, b : b + 1], (PIV, 128)) for b in range(PIV)]
+
+    def wide(c):
+        return jnp.concatenate([c] * (n // 128), axis=1) if n > 128 else c
+
+    def times(cols, tile):
+        return add_up([wide(cols[b]) * jnp.broadcast_to(tile[b : b + 1, :], (PIV, n)) for b in range(PIV)])
+
+    def within(g, iota):
+        return (iota >= g * PIV) & (iota < g * PIV + PIV)
+
+    def update(tile, cols, w, g):
+        return jnp.where(within(g, lane), 0.0, tile) - times(cols, w)
+
+    def advance(g, tile, block, later):
+        ahead = columns(later, g + 1)
+        mult = columns(later, g)
+        cols = eliminate(list(block) + columns(tile, g + 1))
+        unit = (lane - g * PIV == lax.broadcasted_iota(jnp.int32, (PIV, n), 0)).astype(F32)
+        w = times(cols[:PIV], jnp.where(within(g, lane), unit, tile))
+        new_block = tuple(
+            ahead[b] - add_up([mult[a] * jnp.broadcast_to(cols[PIV + b][a : a + 1, :], (PIV, 128)) for a in range(PIV)])
+            for b in range(PIV)
+        )
+        return w, update(later, mult, w, g), new_block
 
     def bulk(g, w):
         w_ref[rows(g), :] = w
-        inside = (lanes >= g * PIV) & (lanes < g * PIV + PIV)
+        inside = within(g, lanes)
         x = a_ref[...]
-        w_all = w_ref[...]
-        a_ref[...] = jnp.where(inside, 0.0, x) - dot(jnp.where(inside, x, 0.0), w_all, ((1,), (0,)), HIGHEST)
+        a_ref[...] = jnp.where(inside, 0.0, x) - dot(
+            jnp.where(inside, x, 0.0), w_ref[...], ((1,), (0,)), HIGHEST
+        )
         a_ref[rows(g), :] = w
         w_ref[rows(g), :] = jnp.zeros_like(w)
 
     w_ref[...] = jnp.zeros_like(w_ref)
-    w = eliminate(a_ref[0:PIV, :], front(a_ref[0:PIV, :], 0), 0, lane)
-    tile = update(a_ref[PIV : 2 * PIV, :], w, 0)
+    tile = a_ref[0:PIV, :]
+    carry = advance(0, tile, columns(tile, 0), a_ref[PIV : 2 * PIV, :])
 
     def group(g, carry):
-        w, tile = carry
-        later = update(a_ref[rows(lax.rem(g + 1, groups)), :], w, g - 1)
-        fresh = eliminate(tile, front(tile, g), g, lane)
+        w, tile, block = carry
+        later = a_ref[rows(lax.rem(g + 1, groups)), :]
+        later = update(later, columns(later, g - 1), w, g - 1)
+        out = advance(g, tile, block, later)
         bulk(g - 1, w)
-        return fresh, update(later, fresh, g)
-
-    w, _ = lax.fori_loop(1, groups, group, (w, tile))
+        return out
+
+    w = lax.fori_loop(1, groups, group, carry)[0]
     bulk(groups - 1, w)
+
+
+def factor(mat, below, w):
+    h = mat.shape[0] // 2
+    top = mat.at[0:h, 0:h]
+    rest = mat.at[h : 2 * h, h : 2 * h]
+    invert(top, w)
+    below[...] = dot(mat[h : 2 * h, 0:h], top[...], ((1,), (0,)), HIGHEST)
+    rest[...] = rest[...] - dot(below[...], mat[0:h, h : 2 * h], ((1,), (0,)), HIGHEST)
+    invert(rest, w)
+
+
+def solve(rhs, mat, below):
+    h = mat.shape[0] // 2
+    one, two = rhs[:, 0:h], rhs[:, h : 2 * h]
+    two = two - dot(one, below[...], ((1,), (1,)), HIGHEST)
+    two = dot(two, mat[h : 2 * h, h : 2 * h], ((1,), (0,)), HIGHEST)
+    one = dot(one, mat[0:h, 0:h], ((1,), (0,)), HIGHEST) - dot(two, below[...], ((1,), (0,)), HIGHEST)
+    return jnp.concatenate([one, two], axis=1)
 
 
 def helpers(axis, count):
@@ -124,7 +159,7 @@
 
 def kernel(nrow, ncol, share, frames, rf, cf, rhist, chist, tgram, o_f, o_row, o_col,
            slab, cgram, gall, recv, full, hall, hrecv, hfull, rhs, ppart, precv, pfull,
-           total, mat, w, tnew, *sems):
+           total, mat, w, below, tnew, *sems):
     (slab_m, cg_m, rs_m, ag_m, ax_m, rhs_m, gs_m, ga_m, gx_m, ps_m, pa_m) = (
         sems[2 * i : 2 * i + 2] for i in range(11)
     )
@@ -190,19 +225,19 @@
     rhs[row, nb:8, :] = jnp.zeros((8 - nb, rank), F32)
     gram_times(full, tnew, ag_m, ax_m)
     send_r(lambda p: rhs.at[row], rhs, rhs_m)
-    invert(mat, w)
+    factor(mat, below, w)
     wait_r(rhs, rhs_m)
-    ff = dot(total_of(rhs), mat[...], ((1,), (0,)), HIGHEST)
+    ff = solve(total_of(rhs), mat, below)
     o_f[...] = ff[:nb]
 
     time_new = tgram[...] + dot(ff, ff, ((0,), (0,)), HIGHEST)
     mat[...] = time_new * tnew[...]
     tnew[...] = time_new
-    invert(mat, w)
+    factor(mat, below, w)
     sums = rhist[...]
     for b in range(nb):
         sums = sums + ff[b : b + 1, :] * total[b]
-    new_row = dot(sums, mat[...], ((1,), (0,)), HIGHEST).astype(jnp.bfloat16)
+    new_row = solve(sums, mat, below).astype(jnp.bfloat16)
     o_row[...] = new_row
 
     gram_start(new_row, hall, hrecv)
@@ -226,12 +261,12 @@
     gram_times(hfull, tnew, ga_m, gx_m)
     precv[row] = ppart[row]
     send_r(lambda p: ppart.at[p], precv, ps_m)
-    invert(mat, w)
+    factor(mat, below, w)
     wait_r(precv, ps_m)
     own = chist[pl.ds(pl.multiple_of(row * pch, pch), pch), :]
     for i in range(nrow):
         own = own + precv[i].astype(F32)
-    pfull[row] = dot(own, mat[...], ((1,), (0,)), HIGHEST).astype(jnp.bfloat16)
+    pfull[row] = solve(own, mat, below).astype(jnp.bfloat16)
     send_r(lambda p: pfull.at[row], pfull, pa_m)
 
     drain_c(lambda p: cgram.at[col], cgram, cg_m)
@@ -257,6 +292,7 @@
     shape = jax.ShapeDtypeStruct
     counts = [ncol, ncol, nrow, nrow, ncol, nrow, nrow, nrow, ncol, nrow, nrow]
     square = vm((rank, rank), F32)
+    quarter = vm((rank // 2, rank // 2), F32)
     part = vm((nrow, pch, rank), bf)
     gram = [
         vm((nrow * share, ch, rank), F32),
@@ -271,7 +307,7 @@
         scratch_shapes=[
             vm((ncol, nb, rows, rank), F32), vm((ncol, rank, rank), F32), *gram, *gram,
             vm((nrow, 8, rank), F32), part, part, part,
-            vm((nb, rows, rank), F32), square, square, square,
+            vm((nb, rows, rank), F32), square, quarter, quarter, square,
         ] + [pltpu.SemaphoreType.DMA((c,)) for c in counts for _ in range(2)],
         compiler_params=pltpu.CompilerParams(
             collective_id=0, has_side_effects=True, vmem_limit_bytes=48 * 1024 * 1024

time: 95.3 us -> 91.8 us (0.963)
  the two profiles are of different devices: /device:TPU:15 before, /device:TPU:28 now
where the time goes in v5:
time: 91.8 us; the launch traced here: 91.5 us
  Pallas kernels  82.1 us (89%)
  local copies, waits for them, and re-layouts  8.69 us (9%)
    pallas_call x1, Pallas kernels, body(): pl.pallas_call(functools.partial(kernel, nrow, ncol, share), out_shape=(s...  82.1 us
    unnamed x15, local copies, waits for them, and re-layouts  8.69 us

profile of v5, /device:TPU:28, one launch (start us, length us, event | category | flops | bytes accessed | tf_op | source)
XLA Modules:
  0.0 91.5 jit_solution(5760294000637198572)
XLA Ops:
  0.6 0.0 copy-start
  0.6 1.6 %copy-done = bf16[4,256,1024]{2,1,0:T(8,128)(2,1)S(1)} copy-done((bf16[4,256,1024]{2,1,0:T(8,128)(2,1)S(1)}, bf16[4,256,1024]{2,1,0:T(8,128)(2,1)}, u32[]{:S(2)}) %copy-start) | copy-done | bytes 2097176
  2.2 0.0 copy-start.1
  2.2 1.2 %copy-done.1 = f32[1024,256]{1,0:T(8,128)S(1)} copy-done((f32[1024,256]{1,0:T(8,128)S(1)}, f32[1024,256]{1,0:T(8,128)}, u32[]{:S(2)}) %copy-start.1) | copy-done | bytes 1048600
  3.4 0.0 copy-start.2
  3.5 1.0 %copy-done.2 = bf16[1024,256]{1,0:T(8,128)(2,1)S(1)} copy-done((bf16[1024,256]{1,0:T(8,128)(2,1)S(1)}, bf16[1024,256]{1,0:T(8,128)(2,1)}, u32[]{:S(2)}) %copy-start.2) | copy-done | bytes 524312
  4.5 0.0 copy-start.3
  4.5 0.9 %copy-done.3 = f32[256,256]{1,0:T(8,128)S(1)} copy-done((f32[256,256]{1,0:T(8,128)S(1)}, f32[256,256]{1,0:T(8,128)}, u32[]{:S(2)}) %copy-start.3) | copy-done | bytes 262168
  5.4 0.0 copy-start.4
  5.4 0.9 %copy-done.4 = f32[256,256]{1,0:T(8,128)S(1)} copy-done((f32[256,256]{1,0:T(8,128)S(1)}, f32[256,256]{1,0:T(8,128)}, u32[]{:S(2)}) %copy-start.4) | copy-done | bytes 262168
  6.4 0.0 copy-start.5
  6.4 0.9 copy-done.5
  7.3 82.1 %shard_map.85 = (f32[4,256]{1,0:T(4,128)S(1)}, bf16[256,256]{1,0:T(8,128)(2,1)S(1)}, bf16[1024,256]{1,0:T(8,128)(2,1)S(1)}) custom-call(bf16[4,256,1024]{2,1,0:T(8,128)(2,1)S(1)} %copy-done, bf16[256,256]{1,0:T(8,128)(2,1)S(1)} %copy-done.5, bf16[1024,256]{1,0:T(8,128)(2,1)S(1)} %copy-done.2, f32[256,256]{1,0:T(8,128)S(1)} %copy-done.3, ...), custom_call_target="tpu_custom_call" | custom-call | tf_op jit(solution)/shard_map/pallas_call | solution.py:302
  89.4 0.6 copy.12
  90.0 0.7 copy.13
  90.7 0.8 copy.14
Async XLA Ops:
  0.6 1.6 %copy-start = (bf16[4,256,1024]{2,1,0:T(8,128)(2,1)S(1)}, bf16[4,256,1024]{2,1,0:T(8,128)(2,1)}, u32[]{:S(2)}) copy-start(bf16[4,256,1024]{2,1,0:T(8,128)(2,1)} %frames.1) | copy-start | bytes 6291460
  2.2 1.2 %copy-start.1 = (f32[1024,256]{1,0:T(8,128)S(1)}, f32[1024,256]{1,0:T(8,128)}, u32[]{:S(2)}) copy-start(f32[1024,256]{1,0:T(8,128)} %chist.1) | copy-start | bytes 3145732
  3.4 1.0 %copy-start.2 = (bf16[1024,256]{1,0:T(8,128)(2,1)S(1)}, bf16[1024,256]{1,0:T(8,128)(2,1)}, u32[]{:S(2)}) copy-start(bf16[1024,256]{1,0:T(8,128)(2,1)} %cf.1) | copy-start | bytes 1572868
  4.5 0.9 %copy-start.3 = (f32[256,256]{1,0:T(8,128)S(1)}, f32[256,256]{1,0:T(8,128)}, u32[]{:S(2)}) copy-start(f32[256,256]{1,0:T(8,128)} %rhist.1) | copy-start | bytes 786436
  5.4 0.9 %copy-start.4 = (f32[256,256]{1,0:T(8,128)S(1)}, f32[256,256]{1,0:T(8,128)}, u32[]{:S(2)}) copy-start(f32[256,256]{1,0:T(8,128)} %tgram.1) | copy-start | bytes 786436
  6.4 0.9 copy-start.5

commit v6 on v5

--- a/solution.py
+++ b/solution.py
@@ -10,11 +10,19 @@
 MESH = pl.DeviceIdType.MESH
 HIGHEST = lax.Precision.HIGHEST
 F32 = jnp.float32
+VMEM_BYTES = 62 * 1024 * 1024
 PIV = 8
 
 
 def dot(a, b, dims, precision=None):
     return lax.dot_general(a, b, (dims, ((), ())), precision=precision, preferred_element_type=F32)
+
+
+def reciprocal(x):
+    r = pl.reciprocal(x, approx=True)
+    for _ in range(2):
+        r = r + r * (1.0 - x * r)
+    return r
 
 
 def eliminate(cols):
@@ -22,7 +30,7 @@
     sub = lax.broadcasted_iota(jnp.int32, cols[0].shape, 0)
     for k in range(PIV):
         row = [jnp.broadcast_to(c[k : k + 1, :], c.shape) for c in cols]
-        p = 1.0 / row[k]
+        p = reciprocal(row[k])
         ck = cols[k]
         here = sub == k
         for b in range(len(cols)):
@@ -157,8 +165,8 @@
     return sum((ref[i] for i in range(1, ref.shape[0])), ref[0])
 
 
-def kernel(nrow, ncol, share, frames, rf, cf, rhist, chist, tgram, o_f, o_row, o_col,
-           slab, cgram, gall, recv, full, hall, hrecv, hfull, rhs, ppart, precv, pfull,
+def kernel(nrow, ncol, share, frames_h, rf_h, cf_h, rhist_h, chist_h, tgram_h,
+           o_f, o_row, o_col, frames, rf, cf, rhist, chist, tgram, in_s, slab, cgram, gall, recv, full, hall, hrecv, hfull, rhs, ppart, precv, pfull,
            total, mat, w, below, tnew, *sems):
     (slab_m, cg_m, rs_m, ag_m, ax_m, rhs_m, gs_m, ga_m, gx_m, ps_m, pa_m) = (
         sems[2 * i : 2 * i + 2] for i in range(11)
@@ -200,9 +208,19 @@
         if share > 1:
             drain_c(lambda p: whole.at[col], whole, m_x)
 
+    loads = [
+        pltpu.make_async_copy(src, dst, in_s.at[i])
+        for i, (src, dst) in enumerate(
+            [(rf_h, rf), (cf_h, cf), (frames_h, frames), (tgram_h, tgram), (rhist_h, rhist), (chist_h, chist)]
+        )
+    ]
+    for load in loads:
+        load.start()
     greet_r()
     greet_c()
+    loads[0].wait()
     gram_start(rf[...], gall, recv)
+    loads[1].wait()
     cgram[col] = dot(cf[...], cf[...], ((0,), (0,)))
     pl.semaphore_wait(pltpu.get_barrier_semaphore(), nrow + ncol - 2)
     gram_scatter(gall, recv, rs_m)
@@ -212,6 +230,7 @@
         slab[col, b] = dot(frames[b], cf[...], ((1,), (0,)))
         return carry
 
+    loads[2].wait()
     lax.fori_loop(0, nb, slab_one, 0)
     gram_gather(recv, full, rs_m, ag_m)
     send_c(lambda p: slab.at[col], slab, slab_m)
@@ -230,6 +249,8 @@
     ff = solve(total_of(rhs), mat, below)
     o_f[...] = ff[:nb]
 
+    for load in loads[3:]:
+        load.wait()
     time_new = tgram[...] + dot(ff, ff, ((0,), (0,)), HIGHEST)
     mat[...] = time_new * tnew[...]
     tnew[...] = time_new
@@ -267,7 +288,32 @@
     for i in range(nrow):
         own = own + precv[i].astype(F32)
     pfull[row] = solve(own, mat, below).astype(jnp.bfloat16)
-    send_r(lambda p: pfull.at[row], pfull, pa_m)
+
+    inner = 4 if nrow % 4 == 0 else 1
+    outer = nrow // inner
+    group, place = row // inner, lax.rem(row, inner)
+
+    def pass_on(chunk, to, sem):
+        return pltpu.make_async_remote_copy(
+            src_ref=pfull.at[chunk], dst_ref=pfull.at[chunk], send_sem=pa_m[0].at[sem],
+            recv_sem=pa_m[1].at[chunk], device_id={"row": to}, device_id_type=MESH,
+        )
+
+    def across(d):
+        return pass_on(row, lax.rem(group + d, outer) * inner + place, d)
+
+    def within(d, e):
+        chunk = lax.rem(group + outer - d, outer) * inner + place
+        return pass_on(chunk, group * inner + lax.rem(place + e, inner), outer + d * inner + e)
+
+    for d in range(1, outer):
+        across(d).start()
+    for d in range(outer):
+        if d > 0:
+            chunk = lax.rem(group + outer - d, outer) * inner + place
+            pass_on(chunk, lax.rem(row + 1, nrow), 0).wait_recv()
+        for e in range(1, inner):
+            within(d, e).start()
 
     drain_c(lambda p: cgram.at[col], cgram, cg_m)
     drain_c(lambda p: slab.at[col], slab, slab_m)
@@ -275,10 +321,17 @@
     drain_r(lambda p: rhs.at[row], rhs, rhs_m)
     gram_drain(hall, hrecv, hfull, gs_m, ga_m, gx_m)
     drain_r(lambda p: ppart.at[p], precv, ps_m)
-    wait_r(pfull, pa_m)
+    for d in range(outer):
+        for e in range(1, inner):
+            chunk = lax.rem(group + d, outer) * inner + lax.rem(place + e, inner)
+            pass_on(chunk, lax.rem(row + 1, nrow), 0).wait_recv()
     for i in range(nrow):
         o_col[i * pch : (i + 1) * pch, :] = pfull[i]
-    drain_r(lambda p: pfull.at[row], pfull, pa_m)
+    for d in range(outer):
+        if d > 0:
+            across(d).wait_send()
+        for e in range(1, inner):
+            within(d, e).wait_send()
 
 
 def body(nrow, ncol, frames, rf, cf, rhist, chist, tgram):
@@ -290,7 +343,7 @@
     bf = jnp.bfloat16
     space = pl.BlockSpec(memory_space=vm)
     shape = jax.ShapeDtypeStruct
-    counts = [ncol, ncol, nrow, nrow, ncol, nrow, nrow, nrow, ncol, nrow, nrow]
+    counts = [ncol, ncol, nrow, nrow, ncol, nrow, nrow, nrow, ncol, nrow]
     square = vm((rank, rank), F32)
     quarter = vm((rank // 2, rank // 2), F32)
     part = vm((nrow, pch, rank), bf)
@@ -302,15 +355,17 @@
     return pl.pallas_call(
         functools.partial(kernel, nrow, ncol, share),
         out_shape=(shape((nb, rank), F32), shape((rows, rank), bf), shape((cols, rank), bf)),
-        in_specs=[space] * 6,
+        in_specs=[pl.BlockSpec(memory_space=pl.ANY)] * 6,
         out_specs=(space,) * 3,
-        scratch_shapes=[
+        scratch_shapes=[vm(x.shape, x.dtype) for x in (frames, rf, cf, rhist, chist, tgram)] + [
+            pltpu.SemaphoreType.DMA((6,)),
             vm((ncol, nb, rows, rank), F32), vm((ncol, rank, rank), F32), *gram, *gram,
             vm((nrow, 8, rank), F32), part, part, part,
             vm((nb, rows, rank), F32), square, quarter, quarter, square,
-        ] + [pltpu.SemaphoreType.DMA((c,)) for c in counts for _ in range(2)],
+        ] + [pltpu.SemaphoreType.DMA((c,)) for c in counts for _ in range(2)]
+        + [pltpu.SemaphoreType.DMA((2 * nrow + nrow // 4 + 1,)), pltpu.SemaphoreType.DMA((nrow,))],
         compiler_params=pltpu.CompilerParams(
-            collective_id=0, has_side_effects=True, vmem_limit_bytes=48 * 1024 * 1024
+            collective_id=0, has_side_effects=True, vmem_limit_bytes=VMEM_BYTES
         ),
     )(frames, rf, cf, rhist, chist, tgram)
 

time: 91.8 us -> 87.6 us (0.954)
  the two profiles are of different devices: /device:TPU:28 before, /device:TPU:0 now
where the time goes in v6:
time: 87.6 us; the launch traced here: 87.3 us
  Pallas kernels  82 us (94%)
  local copies, waits for them, and re-layouts  4.71 us (5%)
    pallas_call x1, Pallas kernels, body(): pl.pallas_call(functools.partial(kernel, nrow, ncol, share), out_shape=(s...  82 us
    unnamed x3, local copies, waits for them, and re-layouts  4.71 us

profile of v6, /device:TPU:0, one launch (start us, length us, event | category | flops | bytes accessed | tf_op | source)
XLA Modules:
  0.0 87.3 jit_solution(9390024893300201216)
XLA Ops:
  0.6 82.0 %shard_map.85 = (f32[4,256]{1,0:T(4,128)}, bf16[256,256]{1,0:T(8,128)(2,1)}, bf16[1024,256]{1,0:T(8,128)(2,1)}) custom-call(bf16[4,256,1024]{2,1,0:T(8,128)(2,1)} %frames_h.1, bf16[256,256]{1,0:T(8,128)(2,1)} %rf_h.1, bf16[1024,256]{1,0:T(8,128)(2,1)} %cf_h.1, f32[256,256]{1,0:T(8,128)} %rhist_h.1, f32[1024,256]{1,0:T(8,128)} %chist_h.1, f32[256,256]{1,0:T(8,128)} %tgram_h.1), custom_call_target="tpu_custom_call" | custom-call | tf_op jit(solution)/shard_map/pallas_call | solution.py:355
  82.6 1.3 %copy.12 = f32[4,256]{1,0:T(4,128)} copy(f32[4,256]{1,0:T(4,128)} %get-tuple-element.6) | data formatting | bytes 8192
  83.9 1.6 %copy.13 = bf16[256,256]{1,0:T(8,128)(2,1)} copy(bf16[256,256]{1,0:T(8,128)(2,1)} %get-tuple-element.7) | data formatting | bytes 262144
  85.5 1.9 %copy.14 = bf16[1024,256]{1,0:T(8,128)(2,1)} copy(bf16[1024,256]{1,0:T(8,128)(2,1)} %get-tuple-element.8) | data formatting | bytes 1048576

commit v7 on v6

--- a/solution.py
+++ b/solution.py
@@ -10,7 +10,7 @@
 MESH = pl.DeviceIdType.MESH
 HIGHEST = lax.Precision.HIGHEST
 F32 = jnp.float32
-VMEM_BYTES = 62 * 1024 * 1024
+VMEM_BYTES = 61 * 1024 * 1024
 PIV = 8
 
 

time: 87.6 us -> 87.6 us (level)
  no operation moved by 1% of the time
where the time goes in v7:
time: 87.6 us; the launch traced here: 87.3 us
  Pallas kernels  82 us (94%)
  local copies, waits for them, and re-layouts  4.71 us (5%)
    pallas_call x1, Pallas kernels, body(): pl.pallas_call(functools.partial(kernel, nrow, ncol, share), out_shape=(s...  82 us
    unnamed x3, local copies, waits for them, and re-layouts  4.71 us

profile of v7, /device:TPU:0, one launch (start us, length us, event | category | flops | bytes accessed | tf_op | source)
XLA Modules:
  0.0 87.3 jit_solution(9390024893300201216)
XLA Ops:
  0.6 82.0 %shard_map.85 = (f32[4,256]{1,0:T(4,128)}, bf16[256,256]{1,0:T(8,128)(2,1)}, bf16[1024,256]{1,0:T(8,128)(2,1)}) custom-call(bf16[4,256,1024]{2,1,0:T(8,128)(2,1)} %frames_h.1, bf16[256,256]{1,0:T(8,128)(2,1)} %rf_h.1, bf16[1024,256]{1,0:T(8,128)(2,1)} %cf_h.1, f32[256,256]{1,0:T(8,128)} %rhist_h.1, f32[1024,256]{1,0:T(8,128)} %chist_h.1, f32[256,256]{1,0:T(8,128)} %tgram_h.1), custom_call_target="tpu_custom_call" | custom-call | tf_op jit(solution)/shard_map/pallas_call | solution.py:355
  82.6 1.3 %copy.12 = f32[4,256]{1,0:T(4,128)} copy(f32[4,256]{1,0:T(4,128)} %get-tuple-element.6) | data formatting | bytes 8192
  83.9 1.6 %copy.13 = bf16[256,256]{1,0:T(8,128)(2,1)} copy(bf16[256,256]{1,0:T(8,128)(2,1)} %get-tuple-element.7) | data formatting | bytes 262144
  85.5 1.9 %copy.14 = bf16[1024,256]{1,0:T(8,128)(2,1)} copy(bf16[1024,256]{1,0:T(8,128)(2,1)} %get-tuple-element.8) | data formatting | bytes 1048576
